TPU v7x, 128 devices: a whole 4x4x4 slice. The times are simulated.
128 devices in a mesh: grp: 2 (over y_hi), ep: 32 (over x, y_lo, z), tp: 2 (over core).
Axes of the slice: x: 4, y: 4 (y_hi: 2, y_lo: 2; y = y_hi * 2 + y_lo), z: 4, core: 2. Of those that a mesh axis runs over, the one named last changes fastest.
Arguments:
- tokens: bfloat16 [1024, 4096], P(('grp', 'ep', 'tp')), may hold values from -6 to 6
- teacher_gain: float32 [4096], replicated, may hold values from 0.1 to 1.9
- student_gain: float32 [4096], replicated, may hold values from 0.1 to 1.9
- expert_ids: int32 [1024, 8], P(('grp', 'ep', 'tp')), may hold values from 0 to 63, all different within a row; in each aligned block of 8 rows (0 to 7, 8 to 15, ...) at most 2 rows name the same one
- route_weights: float32 [1024, 8], P(('grp', 'ep', 'tp')), may hold values from 0.05 to 0.5
- expert_gate: bfloat16 [64, 4096, 768], P(('grp', 'ep'), None, 'tp'), may hold values from -0.09375 to 0.09375
- expert_up: bfloat16 [64, 4096, 768], P(('grp', 'ep'), None, 'tp'), may hold values from -0.09375 to 0.09375
- expert_down: bfloat16 [64, 768, 4096], P(('grp', 'ep'), 'tp'), may hold values from -0.21875 to 0.21875
- student_gate: bfloat16 [4096, 14336], P(None, ('ep', 'tp')), may hold values from -0.09375 to 0.09375
- student_up: bfloat16 [4096, 14336], P(None, ('ep', 'tp')), may hold values from -0.09375 to 0.09375
- student_down: bfloat16 [14336, 4096], P(('ep', 'tp')), may hold values from -0.046875 to 0.046875
Outputs:
- gate_grad: bfloat16 [4096, 14336], P(None, ('ep', 'tp'))
- up_grad: bfloat16 [4096, 14336], P(None, ('ep', 'tp'))
- down_grad: bfloat16 [14336, 4096], P(('ep', 'tp'))
Inputs may be any that keep to these rules, and one draw needn't show every extreme that they name: `expert_ids`: each token names 8 different experts. The tokens of one device name one expert at most 2 times, and in every draw some device names some expert exactly 2 times.
All inputs are finite; a program needn't handle non-finite values.
Results may differ from a plain program's by a relative error of at most 0.011.
Values may be sent and summed in bfloat16 or wider, within the bound.
A program may use at most 128 MiB of HBM per device.

v0:
```python
import math

import jax
import jax.numpy as jnp
from jax import lax
from jax.sharding import PartitionSpec as P

EPSILON = 1e-06


def normalize(values, gain):
    wide = values.astype(jnp.float32)
    scaled = wide * lax.rsqrt(jnp.mean(wide * wide, axis=-1, keepdims=True) + EPSILON)
    return (scaled * gain).astype(jnp.bfloat16)


def route_tables(expert_ids, route_weights, experts, capacity):
    tok_count, choose = expert_ids.shape
    flat_ids = expert_ids.reshape(-1)
    hits = (flat_ids[:, None] == jnp.arange(experts, dtype=jnp.int32)[None, :]).astype(jnp.int32)
    before = jnp.cumsum(hits, axis=0) - hits
    position = jnp.sum(before * hits, axis=1)
    target_slot = flat_ids * capacity + position
    placed = (
        target_slot[:, None] == jnp.arange(experts * capacity, dtype=jnp.int32)[None, :]
    ).astype(jnp.float32)
    owner = jnp.arange(tok_count * choose, dtype=jnp.int32) // choose
    token_hits = (owner[:, None] == jnp.arange(tok_count, dtype=jnp.int32)[None, :]).astype(
        jnp.float32
    )
    picker = jnp.dot(placed.T, token_hits, precision=lax.Precision.HIGHEST).astype(jnp.bfloat16)
    mixer = jnp.dot(
        token_hits.T, placed * route_weights.reshape(-1)[:, None], precision=lax.Precision.HIGHEST
    )
    return (picker, mixer)


def expert_rows(rows, gate_w, up_w, down_w):
    gate_pre = jnp.dot(rows, gate_w, preferred_element_type=jnp.float32)
    up_pre = jnp.dot(rows, up_w, preferred_element_type=jnp.float32)
    hidden = (jax.nn.silu(gate_pre) * up_pre).astype(jnp.bfloat16)
    return jnp.dot(hidden, down_w, preferred_element_type=jnp.float32)


def body(
    tokens,
    teacher_gain,
    student_gain,
    expert_ids,
    route_weights,
    expert_gate,
    expert_up,
    expert_down,
    student_gate,
    student_up,
    student_down,
):
    tok_count, width = tokens.shape
    experts = lax.axis_size(("grp", "ep"))
    lanes = lax.axis_size("tp")
    devices = lax.axis_size(("grp", "ep", "tp"))
    choose = expert_ids.shape[1]
    capacity = max(2, 2 * tok_count * choose // experts)
    teacher_in = normalize(tokens, teacher_gain)
    picker, mixer = route_tables(expert_ids, route_weights, experts, capacity)
    outgoing = jnp.dot(picker, teacher_in, preferred_element_type=jnp.float32).astype(jnp.bfloat16)
    gate_w = expert_gate[0]
    up_w = expert_up[0]
    down_w = expert_down[0]
    copies = jnp.broadcast_to(
        outgoing.reshape(experts, 1, capacity, width), (experts, lanes, capacity, width)
    )
    copies = copies.reshape(experts * lanes, capacity, width)
    arrived = lax.all_to_all(copies, ("grp", "ep", "tp"), split_axis=0, concat_axis=0, tiled=True)
    partial_value = expert_rows(arrived.reshape(-1, width), gate_w, up_w, down_w).astype(
        jnp.bfloat16
    )
    returned = lax.all_to_all(
        partial_value.reshape(devices, capacity, width),
        ("grp", "ep", "tp"),
        split_axis=0,
        concat_axis=0,
        tiled=True,
    )
    halves = returned.reshape(experts, lanes, capacity, width).astype(jnp.float32)
    slots = jnp.sum(halves, axis=1).astype(jnp.bfloat16)
    slots = lax.optimization_barrier(slots).astype(jnp.float32)
    target = jnp.dot(
        mixer, slots.reshape(experts * capacity, width), precision=lax.Precision.HIGHEST
    )
    student_in = normalize(tokens, student_gain)
    gathered = lax.all_gather(student_in, ("ep", "tp"), axis=0, tiled=True)
    gate_pre = jnp.dot(gathered, student_gate, preferred_element_type=jnp.float32)
    up_pre = jnp.dot(gathered, student_up, preferred_element_type=jnp.float32)
    sigma = jax.nn.sigmoid(gate_pre)
    active = gate_pre * sigma
    hidden = (active * up_pre).astype(jnp.bfloat16)
    scale = 1.0 / math.sqrt(tok_count * devices)
    partial_out = jnp.dot(hidden, student_down, preferred_element_type=jnp.float32)
    offset = lax.axis_index(("ep", "tp")) * tok_count
    own_rows = lax.dynamic_update_slice_in_dim(jnp.zeros_like(partial_out), target, offset, 0)
    error = lax.psum(partial_out - own_rows, ("ep", "tp"))
    grad_out = (error * scale).astype(jnp.bfloat16)
    grad_hidden = lax.dot_general(
        grad_out, student_down, (((1,), (1,)), ((), ())), preferred_element_type=jnp.float32
    )
    grad_gate_pre = (grad_hidden * up_pre * sigma * (1.0 + gate_pre * (1.0 - sigma))).astype(
        jnp.bfloat16
    )
    grad_up_pre = (grad_hidden * gate_pre * sigma).astype(jnp.bfloat16)
    gate_acc = lax.dot_general(
        gathered, grad_gate_pre, (((0,), (0,)), ((), ())), preferred_element_type=jnp.float32
    )
    up_acc = lax.dot_general(
        gathered, grad_up_pre, (((0,), (0,)), ((), ())), preferred_element_type=jnp.float32
    )
    down_acc = lax.dot_general(
        hidden, grad_out, (((0,), (0,)), ((), ())), preferred_element_type=jnp.float32
    )
    totals = (
        lax.psum(gate_acc.astype(jnp.bfloat16), "grp").astype(jnp.float32),
        lax.psum(up_acc.astype(jnp.bfloat16), "grp").astype(jnp.float32),
        lax.psum(down_acc.astype(jnp.bfloat16), "grp").astype(jnp.float32),
    )
    return (
        totals[0].astype(jnp.bfloat16),
        totals[1].astype(jnp.bfloat16),
        totals[2].astype(jnp.bfloat16),
    )


def solution(mesh):
    in_specs = (
        P(("grp", "ep", "tp"), None),
        P(),
        P(),
        P(("grp", "ep", "tp"), None),
        P(("grp", "ep", "tp"), None),
        P(("grp", "ep"), None, "tp"),
        P(("grp", "ep"), None, "tp"),
        P(("grp", "ep"), "tp", None),
        P(None, ("ep", "tp")),
        P(None, ("ep", "tp")),
        P(("ep", "tp"), None),
    )
    out_specs = (P(None, ("ep", "tp")), P(None, ("ep", "tp")), P(("ep", "tp"), None))
    return jax.shard_map(body, mesh=mesh, in_specs=in_specs, out_specs=out_specs, check_vma=False)
```

profile of v0, /device:TPU:1, one launch (start us, length us, event | category | flops | bytes accessed | tf_op | source)
XLA Modules:
  0.0 912.0 jit_solution(11740750880126867407)
XLA Ops:
  7.2 1.1 fusion.26
  8.4 1.6 fusion.24
  10.0 0.8 reshape.59
  11.1 0.3 convolution_convert_fusion.5
  11.4 2.3 convolution_convert_fusion.4
  13.7 2.5 broadcast_in_dim.7
  16.2 3.7 broadcast_in_dim.8
  19.9 44.5 %all_to_all.10 = bf16[128,2,4096]{2,1,0:T(2,128)(2,1)} all-to-all(bf16[128,2,4096]{2,1,0:T(2,128)(2,1)S(1)} %bitcast.33), channel_id=1, replica_groups=mesh['grp'=2,'ep'=32,'tp'=2] {'grp','ep','tp'}, dimensions={0} | all-to-all | bytes 4194304 | tf_op jit(solution)/shard_map/all_to_all | solution.py:74
  64.4 4.1 reshape.61
  68.5 3.8 fusion.3
  72.4 6.3 convolution_convert_fusion
  78.7 4.4 reshape.62
  83.1 5.0 all-to-all-start.1
  88.7 32.4 %all-to-all-done.1 = bf16[128,2,4096]{2,1,0:T(2,128)(2,1)S(1)} async-done(((bf16[128,2,4096]{2,1,0:T(2,128)(2,1)}), bf16[128,2,4096]{2,1,0:T(2,128)(2,1)S(1)}, u32[]{:S(2)}, u32[]{:S(2)}) %all-to-all-start.1) | async-done | bytes 2097184 | tf_op jit(solution)/shard_map/all_to_all | solution.py:78
  121.1 2.8 bitcast_reduce_fusion
  123.9 0.4 reshape.64
  124.4 4.3 broadcast_in_dim.6
  128.6 1.2 convolution_dynamic-update-slice_fusion
  129.8 22.9 %all-gather.2.cloned.1.call-done = bf16[512,4096]{1,0:T(8,128)(2,1)} async-done(((bf16[8,4096]{1,0:T(8,128)(2,1)}), bf16[512,4096]{1,0:T(8,128)(2,1)}) %all-gather.2.cloned.1.call-update) | async-done | bytes 4194320 | tf_op jit(solution)/shard_map/all_gather | solution.py:92
  152.7 3.8 fusion.45
  156.7 2.2 multiply_convert_fusion.5
  158.9 7.9 convolution_subtract_fusion
  167.1 574.0 %all-reduce.4.cloned.1.call-done = f32[512,4096]{1,0:T(8,128)} async-done(((f32[512,4096]{1,0:T(8,128)}), f32[512,4096]{1,0:T(8,128)}) %all-reduce.4.cloned.1.call-update) | async-done | bytes 8388624 | tf_op jit(solution)/shard_map/psum | solution.py:102
  741.1 5.9 convolution_convert_fusion.3
  747.1 1.5 fusion.5
  748.6 0.7 copy-done.8
  749.4 2.4 convolution_convert_fusion.1
  751.8 2.5 convolution_convert_fusion.2
  754.2 145.7 %all-reduce.6.cloned.1.call-done = (bf16[4096,224]{0,1:T(8,128)(2,1)}, bf16[4096,224]{0,1:T(8,128)(2,1)}, bf16[224,4096]{1,0:T(8,128)(2,1)}) async-done(((bf16[4096,224]{0,1:T(8,128)(2,1)}, bf16[4096,224]{0,1:T(8,128)(2,1)}, bf16[224,4096]{1,0:T(8,128)(2,1)}), (bf16[4096,224]{0,1:T(8,128)(2,1)}, bf16[4096,224]{0,1:T(8,128)(2,1)}, bf16[224,4096]{1,0:T(8,128)(2,1)})) %all-reduce.6.cloned.1.call-update) | async-done | bytes 5505040 | tf_op jit(solution)/shard_map/psum | solution.py:121
  900.0 3.1 copy.19
  903.1 1.2 copy.20
  904.3 1.2 copy.21
  (40 shorter events, 1.8 us)
Async XLA Ops:
  7.2 65.2 %copy-start = (bf16[1,384,4096]{2,1,0:T(8,128)(2,1)S(1)}, bf16[1,384,4096]{2,1,0:T(8,128)(2,1)}, u32[]{:S(2)}) copy-start(bf16[1,384,4096]{2,1,0:T(8,128)(2,1)} %param.18) | copy-start | bytes 9437188
  7.2 145.5 %all-gather.2.cloned.1.call-start = ((), (), s32[]{:S(2)}) async-start(), calls=%async_computation.2 | async-start | bytes 4259840 | tf_op jit(solution)/shard_map/all_gather | solution.py:92
  83.1 5.2 copy-start.6
  83.1 38.0 %all-to-all-start.1 = ((bf16[128,2,4096]{2,1,0:T(2,128)(2,1)}), bf16[128,2,4096]{2,1,0:T(2,128)(2,1)S(1)}, u32[]{:S(2)}, u32[]{:S(2)}) async-start(bf16[128,2,4096]{2,1,0:T(2,128)(2,1)} %reshape.62), calls=%async_computation.1 | async-start | bytes 4194304 | tf_op jit(solution)/shard_map/all_to_all | solution.py:78
  88.1 653.0 %all-reduce.4.cloned.1.call-start = ((), (), s32[]{:S(2)}) async-start(), calls=%async_computation.3 | async-start | bytes 16777216 | tf_op jit(solution)/shard_map/psum | solution.py:102
  124.4 28.3 %copy-start.9 = (bf16[4096,224]{0,1:T(8,128)(2,1)S(1)}, bf16[4096,224]{0,1:T(8,128)(2,1)}, u32[]{:S(2)}) copy-start(bf16[4096,224]{0,1:T(8,128)(2,1)} %param.19) | copy-start | bytes 5505028
  152.7 3.8 copy-start.7
  152.7 4.0 copy-start.10
  156.7 2.2 copy-start.11
  156.7 2.2 copy-start.3
  166.9 733.1 %all-reduce.6.cloned.1.call-start = ((), (), s32[]{:S(2)}) async-start(), calls=%async_computation.4 | async-start | bytes 11010048 | tf_op jit(solution)/shard_map/psum | solution.py:121
  741.1 6.0 copy-start.2
  747.1 2.2 copy-start.8
  747.1 2.3 copy-start.12
  749.4 2.4 copy-start.13
  900.0 3.1 copy-start.5
  900.0 4.3 copy-start.4
  900.0 5.5 copy-start.1
Sparse Core Ops, SparseCore 0:
  10.3 142.3 all-gather.1
  167.0 574.0 all-reduce.3
  754.4 145.5 all-reduce.5
where the time goes:
time: 913 us; the launch traced here: 912 us
  waiting for transfers between devices  775 us (85%)
  blocking collectives  44.5 us (5%)
  matrix products  40.2 us (4%)
  local copies, waits for them, and re-layouts  27 us (3%)
  between operations  13.9 us (2%)
    psum x1, waiting for transfers between devices, body(): error = lax.psum(partial_out - own_rows, ('ep', 'tp'))  574 us
    psum x1, waiting for transfers between devices, body(): lax.psum(gate_acc.astype(jnp.bfloat16), 'grp').astype(jnp.float32)  146 us
    all_to_all x1, blocking collectives, body(): lax.all_to_all(copies, ('grp', 'ep', 'tp'), split_axis=0, concat_axis=0,...  44.5 us
    all_to_all x1, waiting for transfers between devices, body(): lax.all_to_all(partial_value.reshape(devices, capacity, width), ('grp', '...  32.4 us
    all_gather x1, waiting for transfers between devices, body(): gathered = lax.all_gather(student_in, ('ep', 'tp'), axis=0, tiled=True)  22.9 us
  transfers between devices with their start and end apart: 4, of which 4 were waited for; matrix products, arithmetic and copies ran while one was open for 4% of the time, Pallas kernels for 0%

commit v1 on v0

v1 whole, which is shorter than its diff:
```python
import functools
import math

import jax
import jax.numpy as jnp
from jax import lax
from jax.experimental import pallas as pl
from jax.experimental.pallas import tpu as pltpu
from jax.sharding import PartitionSpec as P

EPSILON = 1e-06
D = 4096
HALF = 2048
META = 128
WIDE = HALF + META
TOKENS = 1024
FE = 384
FU = 224
OWN = 112
MESH = pl.DeviceIdType.MESH
ORDERS = ((0, 1, 2), (1, 2, 0), (2, 0, 1))


def parts_of(width):
    lanes = width // 128
    cuts = [0, -(-lanes // 3), -(-lanes // 3) + -(-(lanes - -(-lanes // 3)) // 2), lanes]
    parts = []
    for p in range(3):
        low, high = cuts[p], cuts[p + 1]
        middle = low + (high - low + 1) // 2
        parts.append((low * 128, middle * 128, high * 128))
    return parts


class Place:
    def __init__(self):
        grp, ep, self.core = lax.axis_index("grp"), lax.axis_index("ep"), lax.axis_index("tp")
        self.at = (ep // 8, grp * 2 + (ep // 4) % 2, ep % 4)
        self.sibling = self.device(self.at, 1 - self.core)

    def device(self, at, core):
        x, y, z = at
        return (y // 2, (x * 2 + y % 2) * 4 + z, core)

    def along(self, dim, step):
        return (self.at[dim] + step + 4) % 4

    def neighbour(self, dim, step):
        at = list(self.at)
        at[dim] = self.along(dim, step)
        return self.device(at, self.core)

    def everyone(self):
        return [self.neighbour(dim, step) for dim in range(3) for step in (1, -1)] + [self.sibling]

    def group(self, order, phase, pos):
        index = [None] * 3
        for j, dim in enumerate(order):
            index[dim] = slice(None) if j < phase else (pos if j == phase else self.at[dim])
        return tuple(index)


def greet(place):
    barrier = pltpu.get_barrier_semaphore()
    friends = place.everyone()
    for device in friends:
        pl.semaphore_signal(barrier, inc=1, device_id=device, device_id_type=MESH)
    pl.semaphore_wait(barrier, len(friends))


def remote(src, dst, send, recv, device):
    return pltpu.make_async_remote_copy(
        src_ref=src, dst_ref=dst, send_sem=send, recv_sem=recv, device_id=device, device_id_type=MESH
    )


def gather(place, buf, width, send, recv, core_send, core_recv):
    parts = parts_of(width)
    core = place.core
    started = []

    def copy(p, phase, way, item, pos, cols):
        order = ORDERS[p]
        view = buf.at[(core,) + place.group(order, phase, pos) + (slice(None), pl.ds(cols[0], cols[1] - cols[0]))]
        return remote(
            view, view, send.at[p, phase, way, item], recv.at[p, phase, way, item],
            place.neighbour(order[phase], 1 if way == 0 else -1),
        )

    def across(p, item, pos, cols, plane):
        view = buf.at[(plane,) + place.group(ORDERS[p], 2, pos) + (slice(None), pl.ds(cols[0], cols[1] - cols[0]))]
        return remote(view, view, core_send.at[p, item], core_recv.at[p, item], place.sibling)

    def go(c):
        c.start()
        started.append(c)

    for phase in range(3):
        for p in range(3):
            low, mid, high = parts[p]
            halves = ((low, mid), (mid, high))
            me = place.at[ORDERS[p][phase]]
            for item in range(2):
                for way in range(2):
                    go(copy(p, phase, way, item, me, halves[item if way == 0 else 1 - item]))
            if phase == 2:
                go(across(p, 0, me, (low, high), core))
        for p in range(3):
            low, mid, high = parts[p]
            halves = ((low, mid), (mid, high))
            dim = ORDERS[p][phase]
            for way in range(2):
                pos = place.along(dim, -1 if way == 0 else 1)
                copy(p, phase, way, 0, pos, halves[way]).wait_recv()
                go(copy(p, phase, way, 2, pos, halves[way]))
        for p in range(3):
            low, mid, high = parts[p]
            halves = ((low, mid), (mid, high))
            dim = ORDERS[p][phase]
            for way in range(2):
                pos = place.along(dim, -1 if way == 0 else 1)
                copy(p, phase, way, 1, pos, halves[1 - way]).wait_recv()
                if phase == 2:
                    go(across(p, 1 + way, pos, (low, high), core))
        for p in range(3):
            low, mid, high = parts[p]
            halves = ((low, mid), (mid, high))
            dim = ORDERS[p][phase]
            far = place.along(dim, 2)
            for way in range(2):
                copy(p, phase, way, 2, far, halves[way]).wait_recv()
                if phase == 2:
                    go(across(p, 3 + way, far, halves[way], core))
    for p in range(3):
        low, mid, high = parts[p]
        dim = ORDERS[p][2]
        across(p, 0, place.at[dim], (low, high), 1 - core).wait_recv()
        across(p, 1, place.along(dim, -1), (low, high), 1 - core).wait_recv()
        across(p, 2, place.along(dim, 1), (low, high), 1 - core).wait_recv()
        across(p, 3, place.along(dim, 2), (low, mid), 1 - core).wait_recv()
        across(p, 4, place.along(dim, 2), (mid, high), 1 - core).wait_recv()
    for c in started:
        c.wait_send()


GATHER_SEMS = [
    pltpu.SemaphoreType.DMA((3, 3, 2, 3)),
    pltpu.SemaphoreType.DMA((3, 3, 2, 3)),
    pltpu.SemaphoreType.DMA((3, 5)),
    pltpu.SemaphoreType.DMA((3, 5)),
]


def gather_kernel(rows_ref, buf, other, block, local_sem, pair_send, pair_recv, send, recv, core_send, core_recv):
    place = Place()
    core = place.core
    greet(place)
    pair = remote(rows_ref.at[1 - core], other, pair_send, pair_recv, place.sibling)
    pair.start()
    pair.wait()
    mine, theirs = rows_ref[core], other[...]
    first = jnp.where(core == 0, mine, theirs)
    second = jnp.where(core == 0, theirs, mine)
    block[...] = jnp.concatenate([first, second], axis=0).astype(jnp.bfloat16)
    x, y, z = place.at
    put = pltpu.make_async_copy(block, buf.at[core, x, y, z], local_sem)
    put.start()
    put.wait()
    gather(place, buf, WIDE, send, recv, core_send, core_recv)


def gather_rows(rows):
    return pl.pallas_call(
        gather_kernel,
        out_shape=jax.ShapeDtypeStruct((2, 4, 4, 4, 16, WIDE), jnp.bfloat16),
        in_specs=[pl.BlockSpec(memory_space=pltpu.VMEM)],
        out_specs=pl.BlockSpec(memory_space=pl.ANY),
        scratch_shapes=[
            pltpu.VMEM((8, WIDE), jnp.float32),
            pltpu.VMEM((16, WIDE), jnp.bfloat16),
            pltpu.SemaphoreType.DMA,
            pltpu.SemaphoreType.DMA,
            pltpu.SemaphoreType.DMA,
        ]
        + GATHER_SEMS,
        compiler_params=pltpu.CompilerParams(collective_id=0, has_side_effects=True),
        name="gather_rows",
    )(rows)


RED_PARTS = parts_of(HALF)


def reduce_kernel(
    hid_ref, down_ref, buf, total, pair_buf, block, *rest
):
    recv_bufs = rest[:18]
    local_sem, pair_send, pair_recv, red_send, red_recv, send, recv, core_send, core_recv = rest[18:]
    place = Place()
    core = place.core
    greet(place)
    tile = 256
    started = []

    def multiply(plane):
        @pl.loop(0, HALF // tile)
        def _(t):
            first = pl.multiple_of(t * tile, tile)
            weights = down_ref[plane, :, pl.ds(first, tile)]
            for x in range(4):
                product = jnp.dot(hid_ref[pl.ds(x * 256, 256), :], weights, preferred_element_type=jnp.float32)
                total[plane, x, :, :, :, pl.ds(first, tile)] = product.astype(jnp.bfloat16).reshape(4, 4, 16, tile)

    def pair(part, plane):
        low, _, high = RED_PARTS[part]
        cols = pl.ds(low, high - low)
        return remote(
            total.at[plane, :, :, :, :, cols], pair_buf.at[:, :, :, :, cols],
            pair_send.at[part], pair_recv.at[part], place.sibling,
        )

    multiply(1 - core)
    for p in range(3):
        c = pair(p, 1 - core)
        c.start()
        started.append(c)
    multiply(core)

    def halves_of(p):
        low, mid, high = RED_PARTS[p]
        return ((low, mid), (mid, high))

    def view(p, phase, pos, cols):
        return total.at[(core,) + place.group(ORDERS[p], phase, pos) + (slice(None), pl.ds(cols[0], cols[1] - cols[0]))]

    def box(p, phase, way):
        return recv_bufs[(p * 3 + phase) * 2 + way]

    def spot(p, phase, way, item, cols):
        lead = (slice(None),) * phase
        if phase:
            return box(p, phase, way).at[(item,) + lead + (slice(None), pl.ds(0, cols[1] - cols[0]))]
        return box(p, phase, way).at[item, :, pl.ds(0, cols[1] - cols[0])]

    def send_part(p, phase, way, item, pos, cols):
        return remote(
            view(p, phase, pos, cols), spot(p, phase, way, item, cols),
            red_send.at[p, phase, way, item], red_recv.at[p, phase, way, item],
            place.neighbour(ORDERS[p][phase], 1 if way == 0 else -1),
        )

    def go(c):
        c.start()
        started.append(c)

    def add(p, phase, pos, cols, sources):
        lead = place.group(ORDERS[p], phase, pos)
        whole = [i for i, v in enumerate(lead) if isinstance(v, slice)]
        width = pl.ds(cols[0], cols[1] - cols[0])

        def step(number):
            index = list(lead)
            inner = []
            if len(whole) == 2:
                index[whole[0]], index[whole[1]] = number // 4, number % 4
            elif len(whole) == 1:
                index[whole[0]] = number
            inner = tuple(index[i] for i in whole)
            here = (core,) + tuple(index) + (slice(None), width)
            value = total[here].astype(jnp.float32)
            for source in sources:
                value = value + source[inner + (slice(None), slice(None))].astype(jnp.float32)
            return here, value

        if not whole:
            return step(0)[1]

        @pl.loop(0, 4 ** len(whole))
        def _(number):
            here, value = step(number)
            total[here] = value.astype(jnp.bfloat16)

    for phase in (2, 1, 0):
        for p in range(3):
            dim = ORDERS[p][phase]
            halves = halves_of(p)
            if phase == 2:
                pair(p, 1 - core).wait_recv()
                low, _, high = RED_PARTS[p]
                cols = pl.ds(low, high - low)

                @pl.loop(0, 64)
                def _(n):
                    at = (n // 16, (n // 4) % 4, n % 4, slice(None), cols)
                    total[(core,) + at] = (
                        total[(core,) + at].astype(jnp.float32) + pair_buf[at].astype(jnp.float32)
                    ).astype(jnp.bfloat16)

            for way in range(2):
                go(send_part(p, phase, way, 0, place.along(dim, 2), halves[way]))
            for way in range(2):
                go(send_part(p, phase, way, 1, place.along(dim, 1 if way == 0 else -1), halves[1 - way]))
        for p in range(3):
            dim = ORDERS[p][phase]
            halves = halves_of(p)
            for way in range(2):
                pos = place.along(dim, 1 if way == 0 else -1)
                send_part(p, phase, way, 0, pos, halves[way]).wait_recv()
                value = add(p, phase, pos, halves[way], [spot(p, phase, way, 0, halves[way])])
                if phase == 0:
                    view(p, 0, pos, halves[way])[...] = value.astype(jnp.bfloat16)
                go(send_part(p, phase, way, 2, pos, halves[way]))
        for p in range(3):
            dim = ORDERS[p][phase]
            halves = halves_of(p)
            me = place.at[dim]
            for half in range(2):
                send_part(p, phase, half, 2, me, halves[half]).wait_recv()
                send_part(p, phase, 1 - half, 1, me, halves[half]).wait_recv()
                value = add(
                    p, phase, me, halves[half],
                    [spot(p, phase, half, 2, halves[half]), spot(p, phase, 1 - half, 1, halves[half])],
                )
                if phase == 0:
                    width = pl.ds(halves[half][0], halves[half][1] - halves[half][0])
                    block[:, width] = (value * (1.0 / math.sqrt(TOKENS))).astype(jnp.bfloat16)
    x, y, z = place.at
    put = pltpu.make_async_copy(block, buf.at[core, x, y, z], local_sem)
    put.start()
    put.wait()
    gather(place, buf, HALF, send, recv, core_send, core_recv)
    for c in started:
        c.wait_send()


def reduce_and_gather(hid, down):
    boxes = []
    for p in range(3):
        low, mid, high = RED_PARTS[p]
        for phase in range(3):
            for way in range(2):
                boxes.append(pltpu.VMEM((3,) + (4,) * phase + (16, max(mid - low, high - mid)), jnp.bfloat16))
    return pl.pallas_call(
        reduce_kernel,
        out_shape=jax.ShapeDtypeStruct((2, 4, 4, 4, 16, HALF), jnp.bfloat16),
        in_specs=[pl.BlockSpec(memory_space=pltpu.VMEM)] * 2,
        out_specs=pl.BlockSpec(memory_space=pl.ANY),
        scratch_shapes=[
            pltpu.VMEM((2, 4, 4, 4, 16, HALF), jnp.bfloat16),
            pltpu.VMEM((4, 4, 4, 16, HALF), jnp.bfloat16),
            pltpu.VMEM((16, HALF), jnp.bfloat16),
        ]
        + boxes
        + [
            pltpu.SemaphoreType.DMA,
            pltpu.SemaphoreType.DMA((3,)),
            pltpu.SemaphoreType.DMA((3,)),
            pltpu.SemaphoreType.DMA((3, 3, 2, 3)),
            pltpu.SemaphoreType.DMA((3, 3, 2, 3)),
        ]
        + GATHER_SEMS,
        compiler_params=pltpu.CompilerParams(collective_id=1, has_side_effects=True, vmem_limit_bytes=48 << 20),
        name="reduce_and_gather",
    )(hid, down)


def body(
    tokens, teacher_gain, student_gain, expert_ids, route_weights,
    expert_gate, expert_up, expert_down, student_gate, student_up, student_down,
):
    grp = lax.axis_index("grp")
    expert = grp * 32 + lax.axis_index("ep")
    wide = tokens.astype(jnp.float32)
    scale = lax.rsqrt(jnp.mean(wide * wide, axis=-1, keepdims=True) + EPSILON)
    hits = expert_ids[:, :, None] == jnp.arange(64, dtype=jnp.int32)[None, None, :]
    table = jnp.sum(jnp.where(hits, route_weights[:, :, None], 0.0), axis=1)
    meta = jnp.concatenate([table, jnp.broadcast_to(scale, (8, 64))], axis=1)
    meta_high = meta.astype(jnp.bfloat16).astype(jnp.float32)
    meta_low = (meta - meta_high).astype(jnp.bfloat16).astype(jnp.float32)
    rows = jnp.stack(
        [
            jnp.concatenate([wide[:, :HALF], meta_high], axis=1),
            jnp.concatenate([wide[:, HALF:], meta_low], axis=1),
        ]
    )
    gathered = gather_rows(rows).reshape(2, TOKENS, WIDE)

    def scaled(weights, gain):
        value = (weights.astype(jnp.float32) * gain[:, None]).astype(jnp.bfloat16)
        return jnp.pad(value.reshape(2, HALF, -1), ((0, 0), (0, META), (0, 0)))

    facts = gathered[0, :, HALF:].astype(jnp.float32) + gathered[1, :, HALF:].astype(jnp.float32)
    row_scale = facts[:, 64:65]
    weight = lax.dynamic_slice_in_dim(facts, expert, 1, axis=1)

    def forward(weights, gain):
        pads = scaled(weights, gain)
        return row_scale * (
            jnp.dot(gathered[0], pads[0], preferred_element_type=jnp.float32)
            + jnp.dot(gathered[1], pads[1], preferred_element_type=jnp.float32)
        )

    teacher_gate = forward(expert_gate[0], teacher_gain)
    teacher_up = forward(expert_up[0], teacher_gain)
    teacher_hidden = (jax.nn.silu(teacher_gate) * teacher_up * -weight).astype(jnp.bfloat16)
    gate_pre = forward(student_gate, student_gain)
    up_pre = forward(student_up, student_gain)
    sigma = jax.nn.sigmoid(gate_pre)
    active = gate_pre * sigma
    hidden = (active * up_pre).astype(jnp.bfloat16)
    own = jnp.where(grp == 0, hidden[:, :OWN], hidden[:, OWN:])
    hid = jnp.concatenate([teacher_hidden, jnp.pad(own, ((0, 0), (0, 128 - OWN)))], axis=1)
    own_down = jnp.where(grp == 0, student_down[:OWN], student_down[OWN:])
    down = jnp.concatenate([expert_down[0], jnp.pad(own_down, ((0, 128 - OWN), (0, 0)))], axis=0)
    down = jnp.stack([down[:, :HALF], down[:, HALF:]])
    grad_out = reduce_and_gather(hid, down).reshape(2, TOKENS, HALF)
    grad_hidden = sum(
        lax.dot_general(
            grad_out[h], student_down[:, h * HALF:(h + 1) * HALF], (((1,), (1,)), ((), ())),
            preferred_element_type=jnp.float32,
        )
        for h in range(2)
    )
    grad_gate_pre = (row_scale * grad_hidden * up_pre * sigma * (1.0 + gate_pre * (1.0 - sigma))).astype(jnp.bfloat16)
    grad_up_pre = (row_scale * grad_hidden * active).astype(jnp.bfloat16)

    def input_grad(pre):
        wide = [
            lax.dot_general(gathered[h], pre, (((0,), (0,)), ((), ())), preferred_element_type=jnp.float32)[:HALF]
            for h in range(2)
        ]
        return (jnp.concatenate(wide) * student_gain[:, None]).astype(jnp.bfloat16)

    down_grad = jnp.concatenate(
        [
            lax.dot_general(hidden, grad_out[h], (((0,), (0,)), ((), ())), preferred_element_type=jnp.float32)
            for h in range(2)
        ],
        axis=1,
    ).astype(jnp.bfloat16)
    return input_grad(grad_gate_pre), input_grad(grad_up_pre), down_grad


def solution(mesh):
    everywhere = ("grp", "ep", "tp")
    in_specs = (
        P(everywhere, None),
        P(),
        P(),
        P(everywhere, None),
        P(everywhere, None),
        P(("grp", "ep"), None, "tp"),
        P(("grp", "ep"), None, "tp"),
        P(("grp", "ep"), "tp", None),
        P(None, ("ep", "tp")),
        P(None, ("ep", "tp")),
        P(("ep", "tp"), None),
    )
    out_specs = (P(None, ("ep", "tp")), P(None, ("ep", "tp")), P(("ep", "tp"), None))
    return jax.shard_map(body, mesh=mesh, in_specs=in_specs, out_specs=out_specs, check_vma=False)
```

time: 913 us -> 194 us (0.21)
  waiting for transfers between devices: 775 us -> 0 us
  Pallas kernels: 0 us -> 118 us
  blocking collectives: 44.5 us -> 0 us
  other arithmetic: 5.87 us -> 18.8 us
  between operations: 13.9 us -> 1.1 us
  local copies, waits for them, and re-layouts: 27 us -> 17.5 us
    psum x2 -> x0, waiting for transfers between devices: 720 us -> none  [the longest x1 574 us: body(): error = lax.psum(partial_out - own_rows, ('ep', 'tp'))]
    pallas_call x0 -> x2, Pallas kernels: none -> 118 us  [the longest x1 74.5 us: reduce_and_gather(): pl.pallas_call(reduce_kernel, out_shape=jax.ShapeDtypeStruct((2, 4, 4, 4,...]
    all_to_all x1 -> x0, blocking collectives: 44.5 us -> none  [body(): lax.all_to_all(copies, ('grp', 'ep', 'tp'), split_axis=0, concat_axis=0,...]
    all_to_all x1 -> x0, waiting for transfers between devices: 32.4 us -> none  [body(): lax.all_to_all(partial_value.reshape(devices, capacity, width), ('grp', '...]
    all_gather x1 -> x0, waiting for transfers between devices: 22.9 us -> none  [body(): gathered = lax.all_gather(student_in, ('ep', 'tp'), axis=0, tiled=True)]
    slice x0 -> x5, local copies, waits for them, and re-layouts: none -> 12.8 us  [the longest x1 6.6 us: forward(): gathered[1]]
    broadcast_in_dim x3 -> x1, local copies, waits for them, and re-layouts: 10.5 us -> 0.07 us  [body(): meta = jnp.concatenate([table, jnp.broadcast_to(scale, (8, 64))], axis=1)]
    reshape x4 -> x2, local copies, waits for them, and re-layouts: 9.7 us -> 0.24 us  [scaled(): return jnp.pad(value.reshape(2, HALF, -1), ((0, 0), (0, META), (0, 0)))]
  transfers between devices with their start and end apart: 4 -> 0, of which waited for: 4 -> 0; matrix products, arithmetic and copies ran while one was open for 4% -> 0% of each run, Pallas kernels for 0% -> 0%
where the time goes in v1:
time: 194 us; the launch traced here: 193 us
  Pallas kernels  118 us (61%)
  matrix products  37.8 us (19%)
  other arithmetic  18.8 us (10%)
  local copies, waits for them, and re-layouts  17.5 us (9%)
    pallas_call x1, Pallas kernels, reduce_and_gather(): pl.pallas_call(reduce_kernel, out_shape=jax.ShapeDtypeStruct((2, 4, 4, 4,...  74.5 us
    pallas_call x1, Pallas kernels, gather_rows(): pl.pallas_call(gather_kernel, out_shape=jax.ShapeDtypeStruct((2, 4, 4, 4,...  43.6 us
    dot_general x4, matrix products, forward(): jnp.dot(gathered[1], pads[1], preferred_element_type=jnp.float32)  17.1 us
    dot_general x4, matrix products, forward(): jnp.dot(gathered[0], pads[0], preferred_element_type=jnp.float32)  10.8 us
    convert_element_type x2, other arithmetic, scaled(): value = (weights.astype(jnp.float32) * gain[:, None]).astype(jnp.bfloat16)  7.36 us
    slice x1, local copies, waits for them, and re-layouts, forward(): gathered[1]  6.6 us
    dot_general x4, matrix products, input_grad(): lax.dot_general(gathered[h], pre, (((0,), (0,)), ((), ())), preferred_ele...  4.68 us
    slice x1, local copies, waits for them, and re-layouts, body(): grad_out[h]  4.33 us

profile of v1, /device:TPU:1, one launch (start us, length us, event | category | flops | bytes accessed | tf_op | source)
XLA Modules:
  0.0 193.2 jit_solution(12297622755650356894)
XLA Ops:
  0.6 1.0 multiply_reduce_fusion
  1.7 0.8 select_reduce_fusion
  2.6 0.8 fusion.62
  4.1 43.6 %gather_rows.1 = bf16[2,4,4,4,16,2176]{5,4,3,2,1,0:T(8,128)(2,1)} custom-call(f32[2,8,2176]{2,1,0:T(8,128)} %pad_maximum_fusion.2.rows_ref), custom_call_target="tpu_custom_call" | custom-call | tf_op jit(solution)/shard_map/gather_rows/pallas_call | solution.py:173
  47.7 6.6 %fusion.60 = (bf16[1,4,4,4,16,2176]{5,4,3,2,1,0:T(8,128)(2,1)}, bf16[1,4,4,4,16,2176]{5,4,3,2,1,0:T(8,128)(2,1)S(1)}) fusion(bf16[2,4,4,4,16,2176]{5,4,3,2,1,0:T(8,128)(2,1)} %gather_rows.1), kind=kLoop, calls=%fused_computation.95 | loop fusion | bytes 17825792 | tf_op jit(solution)/shard_map/slice | solution.py:400
  54.3 4.4 %multiply_convert_fusion = (bf16[4096,224]{0,1:T(8,128)(2,1)S(1)}, bf16[4096,224]{0,1:T(8,128)(2,1)S(1)}) fusion(bf16[4096,224]{0,1:T(8,128)(2,1)} %param.20, f32[4096]{0:T(1024)S(1)} %copy-done.9, bf16[4096,224]{0,1:T(8,128)(2,1)} %param.19), kind=kLoop, calls=%fused_computation.20 | loop fusion | flops 5505024 | bytes 7356416 | tf_op jit(solution)/shard_map/convert_element_type | solution.py:389
  58.9 2.3 %fusion.35 = f32[1024,224]{1,0:T(8,128)} fusion(bf16[1024,2176]{1,0:T(8,128)(2,1)S(1)} %bitcast.79, bf16[2,2048,224]{1,2,0:T(8,128)(2,1)S(1)} %bitcast.110), kind=kOutput, calls=%fused_computation.61 | convolution fusion | flops 998244352 | bytes 7208960 | tf_op jit(solution)/shard_map/dot_general | solution.py:399
  61.2 1.1 fusion.59
  62.6 0.9 convert_add_fusion
  63.4 4.3 %fusion.30 = f32[1024,224]{1,0:T(8,128)S(1)} fusion(f32[1024,224]{1,0:T(8,128)} %fusion.35, bf16[1024,2176]{1,0:T(8,128)(2,1)} %bitcast.91, bf16[2,2048,224]{1,2,0:T(8,128)(2,1)} %bitcast.111, f32[1024]{0:T(1024)S(1)} %bitcast.114), kind=kOutput, calls=%fused_computation.51 | convolution fusion | flops 998703104 | bytes 8130560 | tf_op jit(solution)/shard_map/dot_general | solution.py:400
  68.0 1.3 fusion.40
  69.3 1.0 slice-done.6
  70.4 2.8 %multiply_convert_fusion.5 = (bf16[1024,224]{1,0:T(8,128)(2,1)}, f32[1024,224]{1,0:T(8,128)}) fusion(f32[1024,224]{1,0:T(8,128)S(1)} %fusion.30, f32[1024,224]{1,0:T(8,128)S(1)} %fusion.40, bf16[1024,2176]{1,0:T(8,128)(2,1)S(1)} %bitcast.95, bf16[2,2048,224]{1,2,0:T(8,128)(2,1)S(1)} %bitcast.113, f32[1024]{0:T(1024)S(1)} %bitcast.115), kind=kOutput, calls=%fused_computation.57 | convolution fusion | flops 1000079360 | bytes 9506816 | tf_op jit(solution)/shard_map/dot_general | solution.py:400
  73.2 2.0 %slice_select_fusion.1 = bf16[1024,112]{1,0:T(8,128)(2,1)} fusion(bf16[1024,224]{1,0:T(8,128)(2,1)} %get-tuple-element.23, pred[]{:T(512)S(6)} %eq.20), kind=kLoop, calls=%fused_computation.71 | loop fusion | flops 114688 | bytes 688129 | tf_op jit(solution)/shard_map/jit(_where)/select_n | solution.py:411
  75.2 3.0 %fusion.2 = (bf16[2,2048,384]{2,1,0:T(8,128)(2,1)S(1)}, bf16[2,2048,384]{2,1,0:T(8,128)(2,1)S(1)}) fusion(bf16[2,2048,384]{2,1,0:T(8,128)(2,1)S(1)} %bitcast.107, f32[2,2048]{1,0:T(2,128)S(1)} %mul.132, bf16[2,2048,384]{2,1,0:T(8,128)(2,1)} %bitcast.108), kind=kLoop, calls=%fused_computation.5 | loop fusion | flops 9437184 | bytes 12599296 | tf_op jit(solution)/shard_map/convert_element_type | solution.py:389
  78.3 3.6 %fusion.22 = f32[1024,384]{1,0:T(8,128)} fusion(bf16[1024,2176]{1,0:T(8,128)(2,1)S(1)} %bitcast.85, bf16[2,2048,384]{2,1,0:T(8,128)(2,1)S(1)} %get-tuple-element.20), kind=kOutput, calls=%fused_computation.44 | convolution fusion | flops 1711276032 | bytes 9175040 | tf_op jit(solution)/shard_map/dot_general | solution.py:399
  81.9 3.6 %fusion.16 = f32[1024,384]{1,0:T(8,128)} fusion(bf16[1024,2176]{1,0:T(8,128)(2,1)S(1)} %bitcast.86, bf16[2,2048,384]{2,1,0:T(8,128)(2,1)S(1)} %get-tuple-element.19), kind=kOutput, calls=%fused_computation.40 | convolution fusion | flops 1711276032 | bytes 9175040 | tf_op jit(solution)/shard_map/dot_general | solution.py:399
  85.5 3.6 %fusion.19 = f32[1024,384]{1,0:T(8,128)} fusion(bf16[1024,2176]{1,0:T(8,128)(2,1)S(1)} %bitcast.98, bf16[2,2048,384]{2,1,0:T(8,128)(2,1)S(1)} %get-tuple-element.19), kind=kOutput, calls=%fused_computation.42 | convolution fusion | flops 1711276032 | bytes 9175040 | tf_op jit(solution)/shard_map/dot_general | solution.py:400
  89.9 6.4 %multiply_convert_fusion.2 = bf16[1024,384]{1,0:T(8,128)(2,1)S(1)} fusion(f32[1024,384]{1,0:T(8,128)} %fusion.22, f32[1024,384]{1,0:T(8,128)} %fusion.16, f32[1024,384]{1,0:T(8,128)} %fusion.19, bf16[1024,2176]{1,0:T(8,128)(2,1)} %bitcast.92, bf16[2,2048,384]{2,1,0:T(8,128)(2,1)S(1)} %copy-done.4, f32[1024]{0:T(1024)S(1)} %bitcast.118, f32[1024]{0:T(1024)S(1)} %bitcast.116), kind=kOutput, calls=%fused_computation.47 | convolution fusion | flops 1715601408 | bytes 13115392 | tf_op jit(solution)/shard_map/dot_general | solution.py:400
  96.6 1.6 copy-done.2
  99.7 74.5 %reduce_and_gather.1 = bf16[2,4,4,4,16,2048]{5,4,3,2,1,0:T(8,128)(2,1)} custom-call(bf16[1024,512]{1,0:T(8,128)(2,1)S(1)} %fusion.32.hid_ref, bf16[2,512,2048]{2,1,0:T(8,128)(2,1)S(1)} %pad_maximum_fusion.down_ref), custom_call_target="tpu_custom_call" | custom-call | tf_op jit(solution)/shard_map/reduce_and_gather/pallas_call | solution.py:343
  174.2 4.3 %fusion.61 = (bf16[1,4,4,4,16,2048]{5,4,3,2,1,0:T(8,128)(2,1)S(1)}, bf16[1,4,4,4,16,2048]{5,4,3,2,1,0:T(8,128)(2,1)S(1)}) fusion(bf16[2,4,4,4,16,2048]{5,4,3,2,1,0:T(8,128)(2,1)} %reduce_and_gather.1), kind=kLoop, calls=%fused_computation.96 | loop fusion | bytes 16777216 | tf_op jit(solution)/shard_map/slice | solution.py:419
  178.6 1.3 fusion.45
  179.9 1.6 multiply_convert_fusion.3
  182.2 1.2 fusion.4
  183.4 1.2 fusion.8
  184.6 1.2 fusion.6
  185.7 1.2 fusion.10
  186.9 2.6 %fusion.13 = (bf16[4096,224]{0,1:T(8,128)(2,1)}, bf16[4096,224]{0,1:T(8,128)(2,1)}) fusion(f32[2048,224]{0,1:T(8,128)S(1)} %fusion.4, f32[2048,224]{0,1:T(8,128)S(1)} %fusion.8, f32[4096]{0:T(1024)S(1)} %copy-done.9, f32[2048,224]{0,1:T(8,128)S(1)} %fusion.6, f32[2048,224]{0,1:T(8,128)S(1)} %fusion.10), kind=kLoop, calls=%fused_computation.19 | loop fusion | flops 5505024 | bytes 11026432 | tf_op jit(solution)/shard_map/convert_element_type | solution.py:432
  189.6 1.1 convolution_convert_fusion
  190.7 1.1 convolution_convert_fusion.1
  191.8 1.4 pad_maximum_fusion.1
  (74 shorter events, 4.8 us)
Async XLA Ops:
  47.7 6.6 %copy-start.9 = (f32[4096]{0:T(1024)S(1)}, f32[4096]{0:T(1024)}, u32[]{:S(2)}) copy-start(f32[4096]{0:T(1024)} %param.13) | copy-start | bytes 49156
  54.3 4.5 %copy-start = (bf16[1,4,4,4,16,2176]{5,4,3,2,1,0:T(8,128)(2,1)}, bf16[1,4,4,4,16,2176]{5,4,3,2,1,0:T(8,128)(2,1)S(1)}, u32[]{:S(2)}) copy-start(bf16[1,4,4,4,16,2176]{5,4,3,2,1,0:T(8,128)(2,1)S(1)} %get-tuple-element.6) | copy-start | bytes 13369348
  58.8 2.4 %copy-start.5 = (bf16[28,2,8,2048]{3,2,0,1:T(8,128)(2,1)}, bf16[28,2,8,2048]{3,2,0,1:T(8,128)(2,1)S(1)}, u32[]{:S(2)}) copy-start(bf16[28,2,8,2048]{3,2,0,1:T(8,128)(2,1)S(1)} %copy.69) | copy-start | bytes 5505028
  63.4 4.5 %slice-start = ((s8[4456448]{0:T(1024)(128)(4,1)}), s8[4194304]{0:T(1024)(128)(4,1)S(1)}, s32[]{:S(2)}) async-start(s8[4456448]{0:T(1024)(128)(4,1)} %bitcast.80), calls=%async_computation | async-start | bytes 8388608
  63.4 4.5 %slice-start.1 = ((s8[4456448]{0:T(1024)(128)(4,1)}), s8[262144]{0:T(1024)(128)(4,1)S(1)}, s32[]{:S(2)}) async-start(s8[4456448]{0:T(1024)(128)(4,1)} %bitcast.80), calls=%async_computation.1 | async-start | bytes 524288
  67.8 1.5 copy-start.11
  67.8 2.6 %slice-start.6 = ((s8[4456448]{0:T(1024)(128)(4,1)}), s8[4194304]{0:T(1024)(128)(4,1)S(1)}, s32[]{:S(2)}) async-start(s8[4456448]{0:T(1024)(128)(4,1)} %bitcast.93), calls=%async_computation.6 | async-start | bytes 8388608
  68.0 2.4 %slice-start.7 = ((s8[4456448]{0:T(1024)(128)(4,1)}), s8[262144]{0:T(1024)(128)(4,1)S(1)}, s32[]{:S(2)}) async-start(s8[4456448]{0:T(1024)(128)(4,1)} %bitcast.93), calls=%async_computation.7 | async-start | bytes 524288
  70.4 4.8 %copy-start.10 = (f32[4096]{0:T(1024)S(1)}, f32[4096]{0:T(1024)}, u32[]{:S(2)}) copy-start(f32[4096]{0:T(1024)} %param.12) | copy-start | bytes 49156
  70.4 4.8 %copy-start.1 = (bf16[1,4096,384]{2,1,0:T(8,128)(2,1)S(1)}, bf16[1,4096,384]{2,1,0:T(8,128)(2,1)}, u32[]{:S(2)}) copy-start(bf16[1,4096,384]{2,1,0:T(8,128)(2,1)} %param.16) | copy-start | bytes 9437188
  73.2 5.1 %slice-start.2 = ((s8[4456448]{0:T(1024)(128)(4,1)}), s8[262144]{0:T(1024)(128)(4,1)S(1)}, s32[]{:S(2)}) async-start(s8[4456448]{0:T(1024)(128)(4,1)} %bitcast.83), calls=%async_computation.2 | async-start | bytes 524288
  75.2 3.1 %slice-start.3 = ((s8[4456448]{0:T(1024)(128)(4,1)}), s8[4194304]{0:T(1024)(128)(4,1)S(1)}, s32[]{:S(2)}) async-start(s8[4456448]{0:T(1024)(128)(4,1)} %bitcast.83), calls=%async_computation.3 | async-start | bytes 8388608
  78.2 3.7 %copy-start.3 = (bf16[2,2048,384]{2,1,0:T(8,128)(2,1)}, bf16[2,2048,384]{2,1,0:T(8,128)(2,1)S(1)}, u32[]{:S(2)}) copy-start(bf16[2,2048,384]{2,1,0:T(8,128)(2,1)S(1)} %get-tuple-element.20) | copy-start | bytes 9437188
  78.3 7.2 %slice-start.8 = ((s8[4456448]{0:T(1024)(128)(4,1)}), s8[4194304]{0:T(1024)(128)(4,1)S(1)}, s32[]{:S(2)}) async-start(s8[4456448]{0:T(1024)(128)(4,1)} %bitcast.96), calls=%async_computation.8 | async-start | bytes 8388608
  81.9 3.6 %slice-start.9 = ((s8[4456448]{0:T(1024)(128)(4,1)}), s8[262144]{0:T(1024)(128)(4,1)S(1)}, s32[]{:S(2)}) async-start(s8[4456448]{0:T(1024)(128)(4,1)} %bitcast.96), calls=%async_computation.9 | async-start | bytes 524288
  85.5 4.4 %copy-start.4 = (bf16[2,2048,384]{2,1,0:T(8,128)(2,1)S(1)}, bf16[2,2048,384]{2,1,0:T(8,128)(2,1)}, u32[]{:S(2)}) copy-start(bf16[2,2048,384]{2,1,0:T(8,128)(2,1)} %copy-done.3) | copy-start | bytes 9437188
  89.9 6.4 %copy-start.7 = (bf16[1024,112]{1,0:T(8,128)(2,1)S(1)}, bf16[1024,112]{1,0:T(8,128)(2,1)}, u32[]{:S(2)}) copy-start(bf16[1024,112]{1,0:T(8,128)(2,1)} %slice_select_fusion.1) | copy-start | bytes 688132
  89.9 6.6 %copy-start.6 = (bf16[224,4096]{1,0:T(8,128)(2,1)S(1)}, bf16[224,4096]{1,0:T(8,128)(2,1)}, u32[]{:S(2)}) copy-start(bf16[224,4096]{1,0:T(8,128)(2,1)} %param.21) | copy-start | bytes 5505028
  96.3 1.9 copy-start.2
  174.2 5.7 %copy-start.12 = (f32[1024,224]{1,0:T(8,128)S(1)}, f32[1024,224]{1,0:T(8,128)}, u32[]{:S(2)}) copy-start(f32[1024,224]{1,0:T(8,128)} %copy-done.11) | copy-start | bytes 2752516
  174.2 5.7 %copy-start.13 = (f32[1024,224]{1,0:T(8,128)S(1)}, f32[1024,224]{1,0:T(8,128)}, u32[]{:S(2)}) copy-start(f32[1024,224]{1,0:T(8,128)} %get-tuple-element.24) | copy-start | bytes 2752516
  178.6 3.0 %slice-start.10 = ((s8[4456448]{0:T(1024)(128)(4,1)}), s8[4194304]{0:T(1024)(128)(4,1)S(1)}, s32[]{:S(2)}) async-start(s8[4456448]{0:T(1024)(128)(4,1)} %bitcast.99), calls=%async_computation.10 | async-start | bytes 8388608
  178.6 4.8 %slice-start.4 = ((s8[4456448]{0:T(1024)(128)(4,1)}), s8[4194304]{0:T(1024)(128)(4,1)S(1)}, s32[]{:S(2)}) async-start(s8[4456448]{0:T(1024)(128)(4,1)} %bitcast.87), calls=%async_computation.4 | async-start | bytes 8388608
  179.9 2.3 %slice-start.11 = ((s8[4456448]{0:T(1024)(128)(4,1)}), s8[262144]{0:T(1024)(128)(4,1)S(1)}, s32[]{:S(2)}) async-start(s8[4456448]{0:T(1024)(128)(4,1)} %bitcast.99), calls=%async_computation.11 | async-start | bytes 524288
  179.9 3.5 %slice-start.5 = ((s8[4456448]{0:T(1024)(128)(4,1)}), s8[262144]{0:T(1024)(128)(4,1)S(1)}, s32[]{:S(2)}) async-start(s8[4456448]{0:T(1024)(128)(4,1)} %bitcast.87), calls=%async_computation.5 | async-start | bytes 524288
  186.9 2.7 %copy-start.8 = (bf16[1024,224]{1,0:T(8,128)(2,1)S(1)}, bf16[1024,224]{1,0:T(8,128)(2,1)}, u32[]{:S(2)}) copy-start(bf16[1024,224]{1,0:T(8,128)(2,1)} %get-tuple-element.23) | copy-start | bytes 1376260

commit v2 on v0

v2 whole, which is shorter than its diff:
```python
import math

import jax
import jax.numpy as jnp
from jax import lax
from jax.experimental import pallas as pl
from jax.experimental.pallas import tpu as pltpu
from jax.sharding import PartitionSpec as P

EPSILON = 1e-06
D = 4096
HALF = 2048
META = 128
WIDE = HALF + META
TOKENS = 1024
FE = 384
FU = 224
OWN = 112
MESH = pl.DeviceIdType.MESH
ORDERS = ((0, 1, 2), (1, 2, 0), (2, 0, 1))
ROWS_OUT = (0, -1, 1, 2)
ROWS_IN = (2, 1, -1, 0)
STEPS = (1, -1, 2)
IN_PARTS = ((0, 384, 768), (768, 1152, 1536), (1536, 1920, WIDE))
OUT_PARTS = ((0, 384, 768), (768, 1152, 1408), (1408, 1792, HALF))


class Place:
    def __init__(self):
        self.grp, ep, self.core = lax.axis_index("grp"), lax.axis_index("ep"), lax.axis_index("tp")
        self.expert = self.grp * 32 + ep
        self.at = (ep // 8, self.grp * 2 + (ep // 4) % 2, ep % 4)
        self.sibling = self.device(self.at, 1 - self.core)

    def device(self, at, core):
        x, y, z = at
        return (y // 2, (x * 2 + y % 2) * 4 + z, core)

    def along(self, dim, step):
        return (self.at[dim] + step + 4) % 4

    def neighbour(self, dim, step):
        at = list(self.at)
        at[dim] = self.along(dim, step)
        return self.device(at, self.core)

    def block(self, p, step):
        index = list(self.at)
        index[ORDERS[p][0]] = self.along(ORDERS[p][0], step)
        return tuple(index)

    def row(self, p, second, third):
        a, b, d = ORDERS[p]
        index = [None] * 3
        index[a], index[b], index[d] = slice(None), self.along(b, second), self.along(d, third)
        return tuple(index)

    def group(self, p, third):
        a, b, d = ORDERS[p]
        index = [None] * 3
        index[a], index[b], index[d] = slice(None), slice(None), self.along(d, third)
        return tuple(index)


def greet(place):
    friends = [place.neighbour(dim, step) for dim in range(3) for step in STEPS] + [place.sibling]
    barrier = pltpu.get_barrier_semaphore()
    for device in friends:
        pl.semaphore_signal(barrier, inc=1, device_id=device, device_id_type=MESH)
    pl.semaphore_wait(barrier, len(friends))


def remote(src, dst, send, recv, device):
    return pltpu.make_async_remote_copy(
        src_ref=src, dst_ref=dst, send_sem=send, recv_sem=recv, device_id=device, device_id_type=MESH
    )


GATHER_SEMS = [
    pltpu.SemaphoreType.DMA((2, 3, 3)),
    pltpu.SemaphoreType.DMA((2, 3, 3)),
    pltpu.SemaphoreType.DMA((2, 3, 4, 2)),
    pltpu.SemaphoreType.DMA((2, 3, 4, 2)),
    pltpu.SemaphoreType.DMA((2, 3, 4)),
]
REDUCE_SEMS = [
    pltpu.SemaphoreType.DMA((2, 3)),
    pltpu.SemaphoreType.DMA((2, 3, 4, 2, 3)),
    pltpu.SemaphoreType.DMA((2, 3, 3)),
    pltpu.SemaphoreType.DMA((2, 3, 3)),
]


class Gather:
    def __init__(self, place, buf, parts, sems):
        self.place, self.buf, self.parts = place, buf, parts
        self.block_sem, self.row_sem, self.near_sem, self.far_sem, self.across_sem = sems
        self.started = []

    def go(self, copy):
        copy.start()
        self.started.append(copy)

    def view(self, p, index, half=None, plane=None):
        low, mid, high = self.parts[p]
        if half is not None:
            low, high = ((low, mid), (mid, high))[half]
        plane = self.place.core if plane is None else plane
        return self.buf.at[(plane,) + index + (slice(None), pl.ds(low, high - low))]

    def copy(self, view, sem, spot, device):
        return remote(view, view, sem.at[(0,) + spot], sem.at[(1,) + spot], device)

    def block(self, p, i, step):
        view = self.view(p, self.place.block(p, step))
        return self.copy(view, self.block_sem, (p, i), self.place.neighbour(ORDERS[p][0], STEPS[i]))

    def row(self, p, i, step):
        view = self.view(p, self.place.row(p, step, 0))
        return self.copy(view, self.row_sem, (p, i), self.place.neighbour(ORDERS[p][1], STEPS[i]))

    def near(self, p, r, way, step):
        view = self.view(p, self.place.row(p, ROWS_OUT[r], step))
        return self.copy(view, self.near_sem, (p, r, way), self.place.neighbour(ORDERS[p][2], STEPS[way]))

    def far(self, p, r, way, step):
        view = self.view(p, self.place.row(p, ROWS_OUT[r], step), half=way)
        return self.copy(view, self.far_sem, (p, r, way), self.place.neighbour(ORDERS[p][2], STEPS[way]))

    def across(self, p, g, plane):
        view = self.view(p, self.place.group(p, ROWS_OUT[g]), plane=plane)
        return self.copy(view, self.across_sem, (p, g), self.place.sibling)

    def send_blocks(self):
        for i in range(3):
            for p in range(3):
                self.go(self.block(p, i, 0))

    def send_rows(self):
        for p in range(3):
            for i in range(3):
                self.block(p, i, -STEPS[i]).wait_recv()
            for i in range(3):
                self.go(self.row(p, i, 0))
        self.spread(0)

    def spread(self, r):
        for p in range(3):
            for way in range(2):
                self.go(self.near(p, r, way, 0))

    def take_row(self, r):
        i = {-1: 0, 1: 1, 2: 2}[ROWS_OUT[r]]
        for p in range(3):
            self.row(p, i, -STEPS[i]).wait_recv()
        self.spread(r)

    def pass_on(self, r):
        for p in range(3):
            for way in range(2):
                self.near(p, r, way, -STEPS[way]).wait_recv()
                self.go(self.far(p, r, way, -STEPS[way]))

    def take_far(self, r):
        for p in range(3):
            for way in range(2):
                self.far(p, r, way, 2).wait_recv()

    def cross(self, g):
        for p in range(3):
            self.go(self.across(p, g, self.place.core))

    def take_across(self, p, g):
        self.across(p, g, 1 - self.place.core).wait_recv()

    def finish(self):
        for copy in self.started:
            copy.wait_send()


class Reduce:
    def __init__(self, place, total, pair_buf, boxes, row_boxes, block_boxes, sems):
        self.place, self.total, self.pair_buf = place, total, pair_buf
        self.boxes, self.row_boxes, self.block_boxes = boxes, row_boxes, block_boxes
        self.pair_sem, self.ring_sem, self.row_sem, self.block_sem = sems
        self.started = []

    def go(self, copy):
        copy.start()
        self.started.append(copy)

    def halves(self, p):
        low, mid, high = OUT_PARTS[p]
        return ((low, mid - low), (mid, high - mid))

    def pair(self, p):
        low, _, high = OUT_PARTS[p]
        cols = pl.ds(low, high - low)
        return remote(
            self.total.at[1 - self.place.core, :, :, :, :, cols], self.pair_buf.at[:, :, :, :, cols],
            self.pair_sem.at[0, p], self.pair_sem.at[1, p], self.place.sibling,
        )

    def ring(self, p, r, way, item, step, half):
        low, width = self.halves(p)[half]
        view = self.total.at[
            (self.place.core,) + self.place.row(p, ROWS_IN[r], step) + (slice(None), pl.ds(low, width))
        ]
        return remote(
            view, self.boxes[p].at[way, item, r, :, :, pl.ds(0, width)],
            self.ring_sem.at[0, p, r, way, item], self.ring_sem.at[1, p, r, way, item],
            self.place.neighbour(ORDERS[p][2], STEPS[way]),
        )

    def row(self, p, i, step):
        low, _, high = OUT_PARTS[p]
        view = self.total.at[(self.place.core,) + self.place.row(p, step, 0) + (slice(None), pl.ds(low, high - low))]
        return remote(
            view, self.row_boxes.at[i, :, :, pl.ds(low, high - low)],
            self.row_sem.at[0, p, i], self.row_sem.at[1, p, i], self.place.neighbour(ORDERS[p][1], STEPS[i]),
        )

    def block(self, p, i, step):
        low, _, high = OUT_PARTS[p]
        view = self.total.at[(self.place.core,) + self.place.block(p, step) + (slice(None), pl.ds(low, high - low))]
        return remote(
            view, self.block_boxes.at[i, :, pl.ds(low, high - low)],
            self.block_sem.at[0, p, i], self.block_sem.at[1, p, i], self.place.neighbour(ORDERS[p][0], STEPS[i]),
        )

    def add(self, p, row, low, width, sources):
        a = ORDERS[p][0]
        cols = pl.ds(low, width)

        @pl.loop(0, 4)
        def _(n):
            index = list(row)
            index[a] = n
            here = (self.place.core,) + tuple(index) + (slice(None), cols)
            value = self.total[here].astype(jnp.float32)
            for source in sources:
                value = value + source[n].astype(jnp.float32)
            self.total[here] = value.astype(jnp.bfloat16)

    def start_part(self, p):
        for r in range(4):
            for way in range(2):
                self.go(self.ring(p, r, way, 0, 2, way))
            for way in range(2):
                self.go(self.ring(p, r, way, 1, STEPS[way], 1 - way))

    def pass_on(self, r):
        for p in range(3):
            for way in range(2):
                low, width = self.halves(p)[way]
                self.ring(p, r, way, 0, 0, way).wait_recv()
                self.add(
                    p, self.place.row(p, ROWS_IN[r], STEPS[way]), low, width,
                    [self.boxes[p].at[way, 0, r, :, :, pl.ds(0, width)]],
                )
                self.go(self.ring(p, r, way, 2, STEPS[way], way))

    def combine(self, r):
        for p in range(3):
            for half in range(2):
                low, width = self.halves(p)[half]
                self.ring(p, r, half, 2, 0, half).wait_recv()
                self.ring(p, r, 1 - half, 1, 0, half).wait_recv()
                self.add(
                    p, self.place.row(p, ROWS_IN[r], 0), low, width,
                    [
                        self.boxes[p].at[half, 2, r, :, :, pl.ds(0, width)],
                        self.boxes[p].at[1 - half, 1, r, :, :, pl.ds(0, width)],
                    ],
                )
            if ROWS_IN[r]:
                self.go(self.row(p, STEPS.index(ROWS_IN[r]), ROWS_IN[r]))

    def last_row(self):
        for p in range(3):
            low, _, high = OUT_PARTS[p]
            for i in range(3):
                self.row(p, i, 0).wait_recv()
            self.add(
                p, self.place.row(p, 0, 0), low, high - low,
                [self.row_boxes.at[i, :, :, pl.ds(low, high - low)] for i in range(3)],
            )
            for i in range(3):
                self.go(self.block(p, i, STEPS[i]))

    def last_block(self, buf):
        for p in range(3):
            low, _, high = OUT_PARTS[p]
            cols = pl.ds(low, high - low)
            for i in range(3):
                self.block(p, i, 0).wait_recv()
            here = (self.place.core,) + self.place.at + (slice(None), cols)
            value = self.total[here].astype(jnp.float32)
            for i in range(3):
                value = value + self.block_boxes[i, :, cols].astype(jnp.float32)
            buf[here] = (value * (1.0 / math.sqrt(TOKENS))).astype(jnp.bfloat16)

    def finish(self):
        for copy in self.started:
            copy.wait_send()


def gain_rows(gain_ref, number):
    return jnp.broadcast_to(gain_ref[pl.ds(number, 1), :], (128, 128)).T


def step_kernel(
    rows_ref, tgain_ref, sgain_ref, eg, eu, ed, sg, su, sd, gate_out, up_out, down_out,
    x_buf, g_buf, total, pair_buf, w_teacher, w_gate, w_up, down, s_down,
    acc_teacher, acc_gate, acc_up, grad_hidden, hid, hidden, other,
    box0, box1, box2, row_boxes, block_boxes, load_sem, store_sem, first_sem, *sems
):
    place = Place()
    core = place.core
    loads = []
    for q in range(4):
        cut = pl.ds(q * 1024, 1024)
        loads.append(
            [
                pltpu.make_async_copy(eg.at[cut], w_teacher.at[cut, pl.ds(0, FE)], load_sem.at[q, 0]),
                pltpu.make_async_copy(eu.at[cut], w_teacher.at[cut, pl.ds(FE, FE)], load_sem.at[q, 1]),
                pltpu.make_async_copy(sg.at[cut], w_gate.at[cut], load_sem.at[q, 2]),
                pltpu.make_async_copy(su.at[cut], w_up.at[cut], load_sem.at[q, 3]),
            ]
        )
    own_rows = pl.ds(pl.multiple_of(place.grp * OWN, 16), OWN)
    loads.append(
        [
            pltpu.make_async_copy(ed, down.at[pl.ds(0, FE)], load_sem.at[4, 0]),
            pltpu.make_async_copy(sd.at[own_rows], down.at[pl.ds(FE, OWN)], load_sem.at[4, 1]),
            pltpu.make_async_copy(sd, s_down, load_sem.at[4, 2]),
        ]
    )
    for bundle in loads:
        for load in bundle:
            load.start()
    down[FE + OWN:, :] = jnp.zeros((512 - FE - OWN, D), jnp.bfloat16)

    @pl.loop(0, 4)
    def _(x):
        for acc in (acc_teacher, acc_gate, acc_up, grad_hidden):
            acc[x] = jnp.zeros(acc.shape[1:], jnp.float32)

    greet(place)

    first = remote(rows_ref.at[1 - core], other, first_sem.at[0], first_sem.at[1], place.sibling)
    first.start()
    first.wait()
    mine, theirs = rows_ref[core], other[...]
    top = jnp.where(core == 0, mine, theirs)
    bottom = jnp.where(core == 0, theirs, mine)
    x_buf[(core,) + place.at] = jnp.concatenate([top, bottom], axis=0).astype(jnp.bfloat16)

    def scale(q):
        for load in loads[q]:
            load.wait()

        @pl.loop(q * 8, q * 8 + 8)
        def _(n):
            cut = pl.ds(pl.multiple_of(n * 128, 128), 128)
            gain = gain_rows(tgain_ref, n)
            for t in range(2 * FE // 128):
                cols = pl.ds(t * 128, 128)
                w_teacher[cut, cols] = (w_teacher[cut, cols].astype(jnp.float32) * gain).astype(jnp.bfloat16)
            gain = gain_rows(sgain_ref, n)
            gain = jnp.concatenate([gain, gain[:, :FU - 128]], axis=1)
            for w in (w_gate, w_up):
                w[cut] = (w[cut].astype(jnp.float32) * gain).astype(jnp.bfloat16)

    def forward(p, g):
        index = place.group(p, ROWS_OUT[g])
        low, _, high = IN_PARTS[p]
        high = min(high, HALF)
        lhs = [x_buf[(h,) + index + (slice(None), pl.ds(low, high - low))].reshape(256, high - low) for h in range(2)]

        def product(w, cols):
            return sum(
                jnp.dot(lhs[h], w[pl.ds(h * HALF + low, high - low), cols], preferred_element_type=jnp.float32)
                for h in range(2)
            )

        def put(acc, cols, value):
            here = index + (slice(None), cols)
            value = value.reshape(4, 4, 16, value.shape[-1])
            acc[here] = acc[here] + value

        @pl.loop(0, 2 * FE // 256)
        def _(t):
            cols = pl.ds(pl.multiple_of(t * 256, 256), 256)
            put(acc_teacher, cols, product(w_teacher, cols))

        put(acc_gate, slice(None), product(w_gate, slice(None)))
        put(acc_up, slice(None), product(w_up, slice(None)))

    ins = Gather(place, x_buf, IN_PARTS, sems[:5])
    ins.send_blocks()
    scale(0)
    ins.send_rows()
    scale(1)
    ins.take_row(1)
    ins.take_row(2)
    scale(2)
    ins.pass_on(0)
    ins.take_row(3)
    ins.cross(0)
    scale(3)
    ins.pass_on(1)
    for p in range(3):
        ins.take_across(p, 0)
        forward(p, 0)
    ins.pass_on(2)
    ins.pass_on(3)
    ins.cross(1)
    ins.cross(2)
    for g in (1, 2):
        for p in range(3):
            ins.take_across(p, g)
            forward(p, g)
        if g == 1:
            ins.take_far(0)
            ins.take_far(1)
    ins.take_far(2)
    ins.take_far(3)
    ins.cross(3)
    for p in range(3):
        ins.take_across(p, 3)
        forward(p, 3)
    for load in loads[4]:
        load.wait()

    lanes = lax.broadcasted_iota(jnp.int32, (256, META), 1)

    def facts(x):
        known = sum(x_buf[h, x, :, :, :, pl.ds(HALF, META)].astype(jnp.float32) for h in range(2)).reshape(256, META)
        row_scale = jnp.sum(jnp.where(lanes == 64, known, 0.0), axis=1, keepdims=True)
        weight = jnp.sum(jnp.where(lanes == place.expert, known, 0.0), axis=1, keepdims=True)
        return row_scale, weight

    @pl.loop(0, 4)
    def _(x):
        row_scale, weight = facts(x)
        gate = acc_teacher[x, :, :, :, pl.ds(0, FE)].reshape(256, FE) * row_scale
        up = acc_teacher[x, :, :, :, pl.ds(FE, FE)].reshape(256, FE) * row_scale
        value = gate * jax.nn.sigmoid(gate) * up * -weight
        hid[x, :, :, :, pl.ds(0, FE)] = value.astype(jnp.bfloat16).reshape(4, 4, 16, FE)
        gate = acc_gate[x].reshape(256, FU) * row_scale
        up = acc_up[x].reshape(256, FU) * row_scale
        acc_gate[x] = gate.reshape(4, 4, 16, FU)
        acc_up[x] = up.reshape(4, 4, 16, FU)
        value = gate * jax.nn.sigmoid(gate) * up
        hidden[x] = value.astype(jnp.bfloat16).reshape(4, 4, 16, FU)
        own = jnp.where(place.grp == 0, value[:, :OWN], value[:, OWN:])
        own = jnp.concatenate([own, jnp.zeros((256, 128 - OWN), jnp.float32)], axis=1)
        hid[x, :, :, :, pl.ds(FE, 128)] = own.astype(jnp.bfloat16).reshape(4, 4, 16, 128)

    red = Reduce(place, total, pair_buf, (box0, box1, box2), row_boxes, block_boxes, sems[5:9])

    def multiply(p, plane, added):
        low, _, high = OUT_PARTS[p]
        width = high - low
        cols = pl.ds(low, width)
        weights = pl.ds(pl.multiple_of(plane * HALF + low, 128), width)

        @pl.loop(0, 4)
        def _(x):
            value = jnp.dot(hid[x].reshape(256, 512), down[:, weights], preferred_element_type=jnp.float32)
            value = value.reshape(4, 4, 16, width)
            if added:
                value = value + pair_buf[x, :, :, :, cols].astype(jnp.float32)
            total[plane, x, :, :, :, cols] = value.astype(jnp.bfloat16)

    for p in range(3):
        multiply(p, 1 - core, False)
        red.go(red.pair(p))
    for p in range(3):
        red.pair(p).wait_recv()
        multiply(p, core, True)
        red.start_part(p)
    red.pass_on(0)
    red.pass_on(1)
    red.combine(0)
    red.pass_on(2)
    red.combine(1)
    red.pass_on(3)
    red.combine(2)
    red.combine(3)
    red.last_row()
    red.last_block(g_buf)

    def backward(p, g):
        index = place.group(p, ROWS_OUT[g])
        low, _, high = OUT_PARTS[p]
        width = high - low
        value = sum(
            lax.dot_general(
                g_buf[(h,) + index + (slice(None), pl.ds(low, width))].reshape(256, width),
                s_down[:, pl.ds(h * HALF + low, width)], (((1,), (1,)), ((), ())), preferred_element_type=jnp.float32,
            )
            for h in range(2)
        ).reshape(4, 4, 16, FU)
        grad_hidden[index] = grad_hidden[index] + value

    outs = Gather(place, g_buf, OUT_PARTS, sems[9:14])
    outs.send_blocks()
    outs.send_rows()
    outs.take_row(1)
    outs.take_row(2)
    outs.pass_on(0)
    outs.take_row(3)
    outs.cross(0)
    outs.pass_on(1)
    for p in range(3):
        outs.take_across(p, 0)
        backward(p, 0)
    outs.pass_on(2)
    outs.pass_on(3)
    outs.cross(1)
    outs.cross(2)
    for g in (1, 2):
        for p in range(3):
            outs.take_across(p, g)
            backward(p, g)
    for r in range(4):
        outs.take_far(r)
    outs.cross(3)
    for p in range(3):
        outs.take_across(p, 3)
        backward(p, 3)

    @pl.loop(0, 4)
    def _(x):
        row_scale, _ = facts(x)
        gate, up = acc_gate[x].reshape(256, FU), acc_up[x].reshape(256, FU)
        sigma = jax.nn.sigmoid(gate)
        grad = grad_hidden[x].reshape(256, FU) * row_scale
        gate_part = grad * up * sigma * (1.0 + gate * (1.0 - sigma))
        up_part = grad * gate * sigma
        hid[x, :, :, :, pl.ds(0, FU)] = gate_part.astype(jnp.bfloat16).reshape(4, 4, 16, FU)
        hid[x, :, :, :, pl.ds(256, FU)] = up_part.astype(jnp.bfloat16).reshape(4, 4, 16, FU)

    stores = []
    for h in range(2):

        @pl.loop(0, HALF // 256)
        def _(t):
            cols = pl.ds(pl.multiple_of(t * 256, 256), 256)
            rows = x_buf[h, :, :, :, :, cols].reshape(TOKENS, 256)
            value = lax.dot_general(
                rows, hid[...].reshape(TOKENS, 512), (((0,), (0,)), ((), ())), preferred_element_type=jnp.float32
            )
            gain = jnp.concatenate([gain_rows(sgain_ref, h * 16 + t * 2 + i) for i in range(2)], axis=0)
            gain = jnp.concatenate([gain, gain[:, :FU - 128]], axis=1)
            cut = pl.ds(pl.multiple_of(h * HALF + t * 256, 256), 256)
            w_gate[cut] = (value[:, :FU] * gain).astype(jnp.bfloat16)
            w_up[cut] = (value[:, 256:256 + FU] * gain).astype(jnp.bfloat16)

        cut = pl.ds(h * HALF, HALF)
        for i, (buf, out) in enumerate(((w_gate, gate_out), (w_up, up_out))):
            store = pltpu.make_async_copy(buf.at[cut], out.at[cut], store_sem.at[h, i])
            store.start()
            stores.append(store)
    for h in range(2):

        @pl.loop(0, HALF // 256)
        def _(t):
            cols = pl.ds(pl.multiple_of(t * 256, 256), 256)
            value = lax.dot_general(
                hidden[...].reshape(TOKENS, FU), g_buf[h, :, :, :, :, cols].reshape(TOKENS, 256),
                (((0,), (0,)), ((), ())), preferred_element_type=jnp.float32,
            )
            s_down[:, pl.ds(pl.multiple_of(h * HALF + t * 256, 256), 256)] = value.astype(jnp.bfloat16)

        cols = pl.ds(h * HALF, HALF)
        store = pltpu.make_async_copy(s_down.at[:, cols], down_out.at[:, cols], store_sem.at[h, 2])
        store.start()
        stores.append(store)
    ins.finish()
    red.finish()
    outs.finish()
    for store in stores:
        store.wait()


def step(rows, tgain, sgain, eg, eu, ed, sg, su, sd):
    bf16, f32 = jnp.bfloat16, jnp.float32
    vmem, hbm = pl.BlockSpec(memory_space=pltpu.VMEM), pl.BlockSpec(memory_space=pl.ANY)
    return pl.pallas_call(
        step_kernel,
        out_shape=(
            jax.ShapeDtypeStruct((D, FU), bf16),
            jax.ShapeDtypeStruct((D, FU), bf16),
            jax.ShapeDtypeStruct((FU, D), bf16),
        ),
        in_specs=[vmem] * 3 + [hbm] * 6,
        out_specs=[hbm] * 3,
        scratch_shapes=[
            pltpu.VMEM((2, 4, 4, 4, 16, WIDE), bf16),
            pltpu.VMEM((2, 4, 4, 4, 16, HALF), bf16),
            pltpu.VMEM((2, 4, 4, 4, 16, HALF), bf16),
            pltpu.VMEM((4, 4, 4, 16, HALF), bf16),
            pltpu.VMEM((D, 2 * FE), bf16),
            pltpu.VMEM((D, FU), bf16),
            pltpu.VMEM((D, FU), bf16),
            pltpu.VMEM((512, D), bf16),
            pltpu.VMEM((FU, D), bf16),
            pltpu.VMEM((4, 4, 4, 16, 2 * FE), f32),
            pltpu.VMEM((4, 4, 4, 16, FU), f32),
            pltpu.VMEM((4, 4, 4, 16, FU), f32),
            pltpu.VMEM((4, 4, 4, 16, FU), f32),
            pltpu.VMEM((4, 4, 4, 16, 512), bf16),
            pltpu.VMEM((4, 4, 4, 16, FU), bf16),
            pltpu.VMEM((8, WIDE), f32),
        ]
        + [pltpu.VMEM((2, 3, 4, 4, 16, 384), bf16)] * 3
        + [
            pltpu.VMEM((3, 4, 16, HALF), bf16),
            pltpu.VMEM((3, 16, HALF), bf16),
            pltpu.SemaphoreType.DMA((5, 4)),
            pltpu.SemaphoreType.DMA((2, 3)),
            pltpu.SemaphoreType.DMA((2,)),
        ]
        + GATHER_SEMS
        + REDUCE_SEMS
        + GATHER_SEMS,
        compiler_params=pltpu.CompilerParams(collective_id=0, has_side_effects=True, vmem_limit_bytes=63 << 20),
        name="distill",
    )(rows, tgain, sgain, eg, eu, ed, sg, su, sd)


def body(
    tokens, teacher_gain, student_gain, expert_ids, route_weights,
    expert_gate, expert_up, expert_down, student_gate, student_up, student_down,
):
    wide = tokens.astype(jnp.float32)
    scale = lax.rsqrt(jnp.mean(wide * wide, axis=-1, keepdims=True) + EPSILON)
    hits = expert_ids[:, :, None] == jnp.arange(64, dtype=jnp.int32)[None, None, :]
    table = jnp.sum(jnp.where(hits, route_weights[:, :, None], 0.0), axis=1)
    meta = jnp.concatenate([table, jnp.broadcast_to(scale, (8, 64))], axis=1)
    meta_high = lax.reduce_precision(meta, 8, 7)
    rows = jnp.stack(
        [
            jnp.concatenate([wide[:, :HALF], meta_high], axis=1),
            jnp.concatenate([wide[:, HALF:], meta - meta_high], axis=1),
        ]
    )
    return step(
        rows, teacher_gain.reshape(32, 128), student_gain.reshape(32, 128),
        expert_gate[0], expert_up[0], expert_down[0], student_gate, student_up, student_down,
    )


def solution(mesh):
    everywhere = ("grp", "ep", "tp")
    in_specs = (
        P(everywhere, None),
        P(),
        P(),
        P(everywhere, None),
        P(everywhere, None),
        P(("grp", "ep"), None, "tp"),
        P(("grp", "ep"), None, "tp"),
        P(("grp", "ep"), "tp", None),
        P(None, ("ep", "tp")),
        P(None, ("ep", "tp")),
        P(("ep", "tp"), None),
    )
    out_specs = (P(None, ("ep", "tp")), P(None, ("ep", "tp")), P(("ep", "tp"), None))
    return jax.shard_map(body, mesh=mesh, in_specs=in_specs, out_specs=out_specs, check_vma=False)
```

time: 913 us -> 150 us (0.16)
  waiting for transfers between devices: 775 us -> 0 us
  Pallas kernels: 0 us -> 129 us
  blocking collectives: 44.5 us -> 0 us
  matrix products: 40.2 us -> 0 us
  between operations: 13.9 us -> 0.68 us
  local copies, waits for them, and re-layouts: 27 us -> 17.2 us
    psum x2 -> x0, waiting for transfers between devices: 720 us -> none  [the longest x1 574 us: body(): error = lax.psum(partial_out - own_rows, ('ep', 'tp'))]
    pallas_call x0 -> x1, Pallas kernels: none -> 129 us  [step(): pl.pallas_call(step_kernel, out_shape=(jax.ShapeDtypeStruct((D, FU), bf16...]
    all_to_all x1 -> x0, blocking collectives: 44.5 us -> none  [body(): lax.all_to_all(copies, ('grp', 'ep', 'tp'), split_axis=0, concat_axis=0,...]
    dot_general x13 -> x0, matrix products: 40.2 us -> none  [the longest x1 7.9 us: body(): jnp.dot(hidden, student_down, preferred_element_type=jnp.float32)]
    all_to_all x1 -> x0, waiting for transfers between devices: 32.4 us -> none  [body(): lax.all_to_all(partial_value.reshape(devices, capacity, width), ('grp', '...]
    all_gather x1 -> x0, waiting for transfers between devices: 22.9 us -> none  [body(): gathered = lax.all_gather(student_in, ('ep', 'tp'), axis=0, tiled=True)]
    broadcast_in_dim x3 -> x1, local copies, waits for them, and re-layouts: 10.5 us -> 0.07 us  [body(): meta = jnp.concatenate([table, jnp.broadcast_to(scale, (8, 64))], axis=1)]
    reshape x4 -> x0, local copies, waits for them, and re-layouts: 9.7 us -> none  [the longest x1 4.38 us: body(): partial_value.reshape(devices, capacity, width)]
  transfers between devices with their start and end apart: 4 -> 0, of which waited for: 4 -> 0; matrix products, arithmetic and copies ran while one was open for 4% -> 0% of each run, Pallas kernels for 0% -> 0%
where the time goes in v2:
time: 150 us; the launch traced here: 149 us
  Pallas kernels  129 us (86%)
  local copies, waits for them, and re-layouts  17.2 us (11%)
  other arithmetic  2.56 us (2%)
    pallas_call x1, Pallas kernels, step(): pl.pallas_call(step_kernel, out_shape=(jax.ShapeDtypeStruct((D, FU), bf16...  129 us
    unnamed x7, local copies, waits for them, and re-layouts  9.4 us
    pallas_call x2, local copies, waits for them, and re-layouts, step(): pl.pallas_call(step_kernel, out_shape=(jax.ShapeDtypeStruct((D, FU), bf16...  6.93 us

profile of v2, /device:TPU:1, one launch (start us, length us, event | category | flops | bytes accessed | tf_op | source)
XLA Modules:
  0.0 149.5 jit_solution(6787607899078511375)
XLA Ops:
  0.6 1.0 multiply_reduce_fusion
  1.6 0.1 broadcast_in_dim.23
  1.7 0.8 select_reduce_fusion
  2.5 0.1 fusion.1
  2.6 0.8 fusion.2
  3.4 0.0 copy-start.1
  3.4 0.7 pad_maximum_fusion.rows_ref
  4.1 4.0 %copy.18.sg = bf16[4096,224]{1,0:T(8,128)(2,1)} copy(bf16[4096,224]{0,1:T(8,128)(2,1)} %param.19) | data formatting | bytes 3670016 | tf_op args[8]
  8.1 0.0 copy-done.1
  8.1 2.5 %copy.19.su = bf16[4096,224]{1,0:T(8,128)(2,1)} copy(bf16[4096,224]{0,1:T(8,128)(2,1)S(1)} %copy-done.1) | data formatting | bytes 3670016 | tf_op args[9]
  10.6 129.1 %distill.1 = (bf16[4096,224]{1,0:T(8,128)(2,1)}, bf16[4096,224]{1,0:T(8,128)(2,1)}, bf16[224,4096]{1,0:T(8,128)(2,1)}) custom-call(f32[2,8,2176]{2,1,0:T(8,128)} %pad_maximum_fusion.rows_ref, f32[32,128]{1,0:T(8,128)} %bitcast.12, f32[32,128]{1,0:T(8,128)} %bitcast.13, bf16[4096,384]{1,0:T(8,128)(2,1)} %bitcast.9, bf16[4096,384]{1,0:T(8,128)(2,1)} %bitcast.10, ...), custom_call_target="tpu_custom_call" | custom-call | tf_op jit(solution)/shard_map/distill/pallas_call | solution.py:592
  139.6 0.0 copy-start
  139.6 4.2 %copy.20 = bf16[4096,224]{0,1:T(8,128)(2,1)} copy(bf16[4096,224]{1,0:T(8,128)(2,1)} %get-tuple-element.6) | data formatting | bytes 3670016 | tf_op jit(solution)/shard_map/distill/pallas_call | solution.py:592
  143.8 0.0 copy-done
  143.8 2.8 %copy.21 = bf16[4096,224]{0,1:T(8,128)(2,1)} copy(bf16[4096,224]{1,0:T(8,128)(2,1)S(1)} %copy-done) | data formatting | bytes 3670016 | tf_op jit(solution)/shard_map/distill/pallas_call | solution.py:592
  146.6 2.9 %copy.23 = bf16[224,4096]{1,0:T(8,128)(2,1)} copy(bf16[224,4096]{1,0:T(8,128)(2,1)} %get-tuple-element.20) | data formatting | bytes 3670016
  (2 shorter events, 0.0 us)
Async XLA Ops:
  3.4 4.7 %copy-start.1 = (bf16[4096,224]{0,1:T(8,128)(2,1)S(1)}, bf16[4096,224]{0,1:T(8,128)(2,1)}, u32[]{:S(2)}) copy-start(bf16[4096,224]{0,1:T(8,128)(2,1)} %param.20) | copy-start | bytes 5505028
  139.6 4.2 %copy-start = (bf16[4096,224]{1,0:T(8,128)(2,1)S(1)}, bf16[4096,224]{1,0:T(8,128)(2,1)}, u32[]{:S(2)}) copy-start(bf16[4096,224]{1,0:T(8,128)(2,1)} %get-tuple-element.7) | copy-start | bytes 5505028

commit v3 on v2

--- a/solution.py
+++ b/solution.py
@@ -55,6 +55,11 @@
         index[a], index[b], index[d] = slice(None), self.along(b, second), self.along(d, third)
         return tuple(index)
 
+    def slab(self, p, second):
+        index = [slice(None)] * 3
+        index[ORDERS[p][1]] = self.along(ORDERS[p][1], second)
+        return tuple(index)
+
     def group(self, p, third):
         a, b, d = ORDERS[p]
         index = [None] * 3
@@ -67,7 +72,7 @@
     barrier = pltpu.get_barrier_semaphore()
     for device in friends:
         pl.semaphore_signal(barrier, inc=1, device_id=device, device_id_type=MESH)
-    pl.semaphore_wait(barrier, len(friends))
+    return lambda: pl.semaphore_wait(barrier, len(friends))
 
 
 def remote(src, dst, send, recv, device):
@@ -84,7 +89,7 @@
     pltpu.SemaphoreType.DMA((2, 3, 4)),
 ]
 REDUCE_SEMS = [
-    pltpu.SemaphoreType.DMA((2, 3)),
+    pltpu.SemaphoreType.DMA((2, 3, 4)),
     pltpu.SemaphoreType.DMA((2, 3, 4, 2, 3)),
     pltpu.SemaphoreType.DMA((2, 3, 3)),
     pltpu.SemaphoreType.DMA((2, 3, 3)),
@@ -193,12 +198,12 @@
         low, mid, high = OUT_PARTS[p]
         return ((low, mid - low), (mid, high - mid))
 
-    def pair(self, p):
+    def pair(self, p, r):
         low, _, high = OUT_PARTS[p]
-        cols = pl.ds(low, high - low)
+        spot = self.place.slab(p, ROWS_IN[r]) + (slice(None), pl.ds(low, high - low))
         return remote(
-            self.total.at[1 - self.place.core, :, :, :, :, cols], self.pair_buf.at[:, :, :, :, cols],
-            self.pair_sem.at[0, p], self.pair_sem.at[1, p], self.place.sibling,
+            self.total.at[(1 - self.place.core,) + spot], self.pair_buf.at[spot],
+            self.pair_sem.at[0, p, r], self.pair_sem.at[1, p, r], self.place.sibling,
         )
 
     def ring(self, p, r, way, item, step, half):
@@ -242,12 +247,11 @@
                 value = value + source[n].astype(jnp.float32)
             self.total[here] = value.astype(jnp.bfloat16)
 
-    def start_part(self, p):
-        for r in range(4):
-            for way in range(2):
-                self.go(self.ring(p, r, way, 0, 2, way))
-            for way in range(2):
-                self.go(self.ring(p, r, way, 1, STEPS[way], 1 - way))
+    def start_row(self, p, r):
+        for way in range(2):
+            self.go(self.ring(p, r, way, 0, 2, way))
+        for way in range(2):
+            self.go(self.ring(p, r, way, 1, STEPS[way], 1 - way))
 
     def pass_on(self, r):
         for p in range(3):
@@ -310,13 +314,13 @@
 
 
 def step_kernel(
-    rows_ref, tgain_ref, sgain_ref, eg, eu, ed, sg, su, sd, gate_out, up_out, down_out,
-    x_buf, g_buf, total, pair_buf, w_teacher, w_gate, w_up, down, s_down,
-    acc_teacher, acc_gate, acc_up, grad_hidden, hid, hidden, other,
-    box0, box1, box2, row_boxes, block_boxes, load_sem, store_sem, first_sem, *sems
+    tokens_ref, ids_ref, weights_ref, tgain_ref, sgain_ref, eg, eu, ed, sg, su, sd, gate_out, up_out, down_out,
+    x_buf, g_buf, total, pair_buf, w_teacher, down, acc_teacher, acc_gate, acc_up, grad_hidden,
+    hid, hidden_t, pre_t, rows, other, box0, box1, box2, row_boxes, block_boxes, load_sem, first_sem, *sems
 ):
     place = Place()
     core = place.core
+    greeted = greet(place)
     loads = []
     for q in range(4):
         cut = pl.ds(q * 1024, 1024)
@@ -324,8 +328,8 @@
             [
                 pltpu.make_async_copy(eg.at[cut], w_teacher.at[cut, pl.ds(0, FE)], load_sem.at[q, 0]),
                 pltpu.make_async_copy(eu.at[cut], w_teacher.at[cut, pl.ds(FE, FE)], load_sem.at[q, 1]),
-                pltpu.make_async_copy(sg.at[cut], w_gate.at[cut], load_sem.at[q, 2]),
-                pltpu.make_async_copy(su.at[cut], w_up.at[cut], load_sem.at[q, 3]),
+                pltpu.make_async_copy(sg.at[:, cut], gate_out.at[:, cut], load_sem.at[q, 2]),
+                pltpu.make_async_copy(su.at[:, cut], up_out.at[:, cut], load_sem.at[q, 3]),
             ]
         )
     own_rows = pl.ds(pl.multiple_of(place.grp * OWN, 16), OWN)
@@ -333,12 +337,24 @@
         [
             pltpu.make_async_copy(ed, down.at[pl.ds(0, FE)], load_sem.at[4, 0]),
             pltpu.make_async_copy(sd.at[own_rows], down.at[pl.ds(FE, OWN)], load_sem.at[4, 1]),
-            pltpu.make_async_copy(sd, s_down, load_sem.at[4, 2]),
+            pltpu.make_async_copy(sd, down_out, load_sem.at[4, 2]),
         ]
     )
     for bundle in loads:
         for load in bundle:
             load.start()
+
+    wide = tokens_ref[...].astype(jnp.float32)
+    scale_own = lax.rsqrt(jnp.mean(wide * wide, axis=-1, keepdims=True) + EPSILON)
+    lane = lax.broadcasted_iota(jnp.int32, (8, META), 1)
+    meta = jnp.where(lane >= 64, scale_own, 0.0)
+    for k in range(8):
+        meta = meta + jnp.where(lane == ids_ref[:, k:k + 1], weights_ref[:, k:k + 1], 0.0)
+    meta_high = meta.astype(jnp.bfloat16).astype(jnp.float32)
+    for h in range(2):
+        rows[h, :, :HALF] = wide[:, h * HALF:(h + 1) * HALF]
+    rows[0, :, HALF:] = meta_high
+    rows[1, :, HALF:] = meta - meta_high
     down[FE + OWN:, :] = jnp.zeros((512 - FE - OWN, D), jnp.bfloat16)
 
     @pl.loop(0, 4)
@@ -346,12 +362,11 @@
         for acc in (acc_teacher, acc_gate, acc_up, grad_hidden):
             acc[x] = jnp.zeros(acc.shape[1:], jnp.float32)
 
-    greet(place)
-
-    first = remote(rows_ref.at[1 - core], other, first_sem.at[0], first_sem.at[1], place.sibling)
+    greeted()
+    first = remote(rows.at[1 - core], other, first_sem.at[0], first_sem.at[1], place.sibling)
     first.start()
     first.wait()
-    mine, theirs = rows_ref[core], other[...]
+    mine, theirs = rows[core], other[...]
     top = jnp.where(core == 0, mine, theirs)
     bottom = jnp.where(core == 0, theirs, mine)
     x_buf[(core,) + place.at] = jnp.concatenate([top, bottom], axis=0).astype(jnp.bfloat16)
@@ -367,37 +382,40 @@
             for t in range(2 * FE // 128):
                 cols = pl.ds(t * 128, 128)
                 w_teacher[cut, cols] = (w_teacher[cut, cols].astype(jnp.float32) * gain).astype(jnp.bfloat16)
-            gain = gain_rows(sgain_ref, n)
-            gain = jnp.concatenate([gain, gain[:, :FU - 128]], axis=1)
-            for w in (w_gate, w_up):
-                w[cut] = (w[cut].astype(jnp.float32) * gain).astype(jnp.bfloat16)
-
-    def forward(p, g):
+            gain = sgain_ref[pl.ds(n, 1), :]
+            for w in (gate_out, up_out):
+                w[:, cut] = (w[:, cut].astype(jnp.float32) * gain).astype(jnp.bfloat16)
+
+    def forward(p, g, plane):
         index = place.group(p, ROWS_OUT[g])
         low, _, high = IN_PARTS[p]
-        high = min(high, HALF)
-        lhs = [x_buf[(h,) + index + (slice(None), pl.ds(low, high - low))].reshape(256, high - low) for h in range(2)]
-
-        def product(w, cols):
-            return sum(
-                jnp.dot(lhs[h], w[pl.ds(h * HALF + low, high - low), cols], preferred_element_type=jnp.float32)
-                for h in range(2)
-            )
+        width = min(high, HALF) - low
+        lhs = x_buf[(plane,) + index + (slice(None), pl.ds(low, width))].reshape(256, width)
+        depth = pl.ds(pl.multiple_of(plane * HALF + low, 128), width)
 
         def put(acc, cols, value):
             here = index + (slice(None), cols)
-            value = value.reshape(4, 4, 16, value.shape[-1])
-            acc[here] = acc[here] + value
-
-        @pl.loop(0, 2 * FE // 256)
-        def _(t):
-            cols = pl.ds(pl.multiple_of(t * 256, 256), 256)
-            put(acc_teacher, cols, product(w_teacher, cols))
-
-        put(acc_gate, slice(None), product(w_gate, slice(None)))
-        put(acc_up, slice(None), product(w_up, slice(None)))
+            acc[here] = acc[here] + value.reshape(4, 4, 16, value.shape[-1])
+
+        put(acc_teacher, slice(None), jnp.dot(lhs, w_teacher[depth, :], preferred_element_type=jnp.float32))
+
+        for acc, w in ((acc_gate, gate_out), (acc_up, up_out)):
+            put(
+                acc, slice(None),
+                lax.dot_general(lhs, w[:, depth], (((1,), (1,)), ((), ())), preferred_element_type=jnp.float32),
+            )
 
     ins = Gather(place, x_buf, IN_PARTS, sems[:5])
+
+    def own(g):
+        for p in range(3):
+            forward(p, g, core)
+
+    def theirs_too(g):
+        for p in range(3):
+            ins.take_across(p, g)
+            forward(p, g, 1 - core)
+
     ins.send_blocks()
     scale(0)
     ins.send_rows()
@@ -409,27 +427,24 @@
     ins.take_row(3)
     ins.cross(0)
     scale(3)
+    own(0)
     ins.pass_on(1)
-    for p in range(3):
-        ins.take_across(p, 0)
-        forward(p, 0)
+    theirs_too(0)
     ins.pass_on(2)
     ins.pass_on(3)
     ins.cross(1)
     ins.cross(2)
-    for g in (1, 2):
-        for p in range(3):
-            ins.take_across(p, g)
-            forward(p, g)
-        if g == 1:
-            ins.take_far(0)
-            ins.take_far(1)
+    own(1)
+    own(2)
+    ins.take_far(0)
+    ins.take_far(1)
+    theirs_too(1)
     ins.take_far(2)
     ins.take_far(3)
     ins.cross(3)
-    for p in range(3):
-        ins.take_across(p, 3)
-        forward(p, 3)
+    theirs_too(2)
+    own(3)
+    theirs_too(3)
     for load in loads[4]:
         load.wait()
 
@@ -453,34 +468,36 @@
         acc_gate[x] = gate.reshape(4, 4, 16, FU)
         acc_up[x] = up.reshape(4, 4, 16, FU)
         value = gate * jax.nn.sigmoid(gate) * up
-        hidden[x] = value.astype(jnp.bfloat16).reshape(4, 4, 16, FU)
-        own = jnp.where(place.grp == 0, value[:, :OWN], value[:, OWN:])
-        own = jnp.concatenate([own, jnp.zeros((256, 128 - OWN), jnp.float32)], axis=1)
-        hid[x, :, :, :, pl.ds(FE, 128)] = own.astype(jnp.bfloat16).reshape(4, 4, 16, 128)
+        hidden_t[:, pl.ds(pl.multiple_of(x * 256, 256), 256)] = value.T.astype(jnp.bfloat16)
+        half = jnp.where(place.grp == 0, value[:, :OWN], value[:, OWN:])
+        half = jnp.concatenate([half, jnp.zeros((256, 128 - OWN), jnp.float32)], axis=1)
+        hid[x, :, :, :, pl.ds(FE, 128)] = half.astype(jnp.bfloat16).reshape(4, 4, 16, 128)
 
     red = Reduce(place, total, pair_buf, (box0, box1, box2), row_boxes, block_boxes, sems[5:9])
 
-    def multiply(p, plane, added):
+    def multiply(p, r, plane, added):
         low, _, high = OUT_PARTS[p]
         width = high - low
-        cols = pl.ds(low, width)
+        slab = place.slab(p, ROWS_IN[r])
+        spot = slab + (slice(None), pl.ds(low, width))
         weights = pl.ds(pl.multiple_of(plane * HALF + low, 128), width)
-
-        @pl.loop(0, 4)
-        def _(x):
-            value = jnp.dot(hid[x].reshape(256, 512), down[:, weights], preferred_element_type=jnp.float32)
-            value = value.reshape(4, 4, 16, width)
-            if added:
-                value = value + pair_buf[x, :, :, :, cols].astype(jnp.float32)
-            total[plane, x, :, :, :, cols] = value.astype(jnp.bfloat16)
-
-    for p in range(3):
-        multiply(p, 1 - core, False)
-        red.go(red.pair(p))
-    for p in range(3):
-        red.pair(p).wait_recv()
-        multiply(p, core, True)
-        red.start_part(p)
+        value = jnp.dot(
+            hid[slab + (slice(None), slice(None))].reshape(256, 512), down[:, weights],
+            preferred_element_type=jnp.float32,
+        ).reshape(4, 4, 16, width)
+        if added:
+            value = value + pair_buf[spot].astype(jnp.float32)
+        total[(plane,) + spot] = value.astype(jnp.bfloat16)
+
+    for r in range(4):
+        for p in range(3):
+            multiply(p, r, 1 - core, False)
+            red.go(red.pair(p, r))
+    for r in range(4):
+        for p in range(3):
+            red.pair(p, r).wait_recv()
+            multiply(p, r, core, True)
+            red.start_row(p, r)
     red.pass_on(0)
     red.pass_on(1)
     red.combine(0)
@@ -499,13 +516,20 @@
         value = sum(
             lax.dot_general(
                 g_buf[(h,) + index + (slice(None), pl.ds(low, width))].reshape(256, width),
-                s_down[:, pl.ds(h * HALF + low, width)], (((1,), (1,)), ((), ())), preferred_element_type=jnp.float32,
+                down_out[:, pl.ds(h * HALF + low, width)], (((1,), (1,)), ((), ())),
+                preferred_element_type=jnp.float32,
             )
             for h in range(2)
         ).reshape(4, 4, 16, FU)
         grad_hidden[index] = grad_hidden[index] + value
 
     outs = Gather(place, g_buf, OUT_PARTS, sems[9:14])
+
+    def back(g):
+        for p in range(3):
+            outs.take_across(p, g)
+            backward(p, g)
+
     outs.send_blocks()
     outs.send_rows()
     outs.take_row(1)
@@ -514,23 +538,19 @@
     outs.take_row(3)
     outs.cross(0)
     outs.pass_on(1)
-    for p in range(3):
-        outs.take_across(p, 0)
-        backward(p, 0)
+    back(0)
     outs.pass_on(2)
     outs.pass_on(3)
     outs.cross(1)
     outs.cross(2)
-    for g in (1, 2):
-        for p in range(3):
-            outs.take_across(p, g)
-            backward(p, g)
-    for r in range(4):
-        outs.take_far(r)
+    outs.take_far(0)
+    outs.take_far(1)
+    back(1)
+    outs.take_far(2)
+    outs.take_far(3)
     outs.cross(3)
-    for p in range(3):
-        outs.take_across(p, 3)
-        backward(p, 3)
+    back(2)
+    back(3)
 
     @pl.loop(0, 4)
     def _(x):
@@ -540,80 +560,54 @@
         grad = grad_hidden[x].reshape(256, FU) * row_scale
         gate_part = grad * up * sigma * (1.0 + gate * (1.0 - sigma))
         up_part = grad * gate * sigma
-        hid[x, :, :, :, pl.ds(0, FU)] = gate_part.astype(jnp.bfloat16).reshape(4, 4, 16, FU)
-        hid[x, :, :, :, pl.ds(256, FU)] = up_part.astype(jnp.bfloat16).reshape(4, 4, 16, FU)
-
-    stores = []
+        cols = pl.ds(pl.multiple_of(x * 256, 256), 256)
+        pre_t[pl.ds(0, FU), cols] = gate_part.T.astype(jnp.bfloat16)
+        pre_t[pl.ds(FU, FU), cols] = up_part.T.astype(jnp.bfloat16)
+
     for h in range(2):
-
-        @pl.loop(0, HALF // 256)
-        def _(t):
-            cols = pl.ds(pl.multiple_of(t * 256, 256), 256)
-            rows = x_buf[h, :, :, :, :, cols].reshape(TOKENS, 256)
-            value = lax.dot_general(
-                rows, hid[...].reshape(TOKENS, 512), (((0,), (0,)), ((), ())), preferred_element_type=jnp.float32
+        for t in range(HALF // 512):
+            cols = pl.ds(t * 512, 512)
+            spot = pl.ds(h * HALF + t * 512, 512)
+            value = jnp.dot(
+                pre_t[...], x_buf[h, :, :, :, :, cols].reshape(TOKENS, 512), preferred_element_type=jnp.float32
             )
-            gain = jnp.concatenate([gain_rows(sgain_ref, h * 16 + t * 2 + i) for i in range(2)], axis=0)
-            gain = jnp.concatenate([gain, gain[:, :FU - 128]], axis=1)
-            cut = pl.ds(pl.multiple_of(h * HALF + t * 256, 256), 256)
-            w_gate[cut] = (value[:, :FU] * gain).astype(jnp.bfloat16)
-            w_up[cut] = (value[:, 256:256 + FU] * gain).astype(jnp.bfloat16)
-
-        cut = pl.ds(h * HALF, HALF)
-        for i, (buf, out) in enumerate(((w_gate, gate_out), (w_up, up_out))):
-            store = pltpu.make_async_copy(buf.at[cut], out.at[cut], store_sem.at[h, i])
-            store.start()
-            stores.append(store)
-    for h in range(2):
-
-        @pl.loop(0, HALF // 256)
-        def _(t):
-            cols = pl.ds(pl.multiple_of(t * 256, 256), 256)
-            value = lax.dot_general(
-                hidden[...].reshape(TOKENS, FU), g_buf[h, :, :, :, :, cols].reshape(TOKENS, 256),
-                (((0,), (0,)), ((), ())), preferred_element_type=jnp.float32,
+            first_gain = h * 16 + t * 4
+            gain = jnp.concatenate([sgain_ref[first_gain + i:first_gain + i + 1, :] for i in range(4)], axis=1)
+            gate_out[:, spot] = (value[:FU] * gain).astype(jnp.bfloat16)
+            up_out[:, spot] = (value[FU:] * gain).astype(jnp.bfloat16)
+            value = jnp.dot(
+                hidden_t[...], g_buf[h, :, :, :, :, cols].reshape(TOKENS, 512), preferred_element_type=jnp.float32
             )
-            s_down[:, pl.ds(pl.multiple_of(h * HALF + t * 256, 256), 256)] = value.astype(jnp.bfloat16)
-
-        cols = pl.ds(h * HALF, HALF)
-        store = pltpu.make_async_copy(s_down.at[:, cols], down_out.at[:, cols], store_sem.at[h, 2])
-        store.start()
-        stores.append(store)
+            down_out[:, spot] = value.astype(jnp.bfloat16)
+
     ins.finish()
     red.finish()
     outs.finish()
-    for store in stores:
-        store.wait()
-
-
-def step(rows, tgain, sgain, eg, eu, ed, sg, su, sd):
+
+
+def step(tokens, ids, weights, tgain, sgain, eg, eu, ed, sg, su, sd):
     bf16, f32 = jnp.bfloat16, jnp.float32
     vmem, hbm = pl.BlockSpec(memory_space=pltpu.VMEM), pl.BlockSpec(memory_space=pl.ANY)
     return pl.pallas_call(
         step_kernel,
-        out_shape=(
-            jax.ShapeDtypeStruct((D, FU), bf16),
-            jax.ShapeDtypeStruct((D, FU), bf16),
-            jax.ShapeDtypeStruct((FU, D), bf16),
-        ),
-        in_specs=[vmem] * 3 + [hbm] * 6,
-        out_specs=[hbm] * 3,
+        out_shape=(pltpu.VMEM((FU, D), bf16),) * 3,
+        in_specs=[vmem] * 5 + [hbm] * 6,
+        out_specs=[vmem] * 3,
         scratch_shapes=[
             pltpu.VMEM((2, 4, 4, 4, 16, WIDE), bf16),
             pltpu.VMEM((2, 4, 4, 4, 16, HALF), bf16),
             pltpu.VMEM((2, 4, 4, 4, 16, HALF), bf16),
             pltpu.VMEM((4, 4, 4, 16, HALF), bf16),
             pltpu.VMEM((D, 2 * FE), bf16),
-            pltpu.VMEM((D, FU), bf16),
-            pltpu.VMEM((D, FU), bf16),
             pltpu.VMEM((512, D), bf16),
-            pltpu.VMEM((FU, D), bf16),
             pltpu.VMEM((4, 4, 4, 16, 2 * FE), f32),
             pltpu.VMEM((4, 4, 4, 16, FU), f32),
             pltpu.VMEM((4, 4, 4, 16, FU), f32),
             pltpu.VMEM((4, 4, 4, 16, FU), f32),
             pltpu.VMEM((4, 4, 4, 16, 512), bf16),
-            pltpu.VMEM((4, 4, 4, 16, FU), bf16),
+            pltpu.VMEM((FU, TOKENS), bf16),
+            pltpu.VMEM((2 * FU, TOKENS), bf16),
+            pltpu.VMEM((2, 8, WIDE), f32),
             pltpu.VMEM((8, WIDE), f32),
         ]
         + [pltpu.VMEM((2, 3, 4, 4, 16, 384), bf16)] * 3
@@ -621,37 +615,25 @@
             pltpu.VMEM((3, 4, 16, HALF), bf16),
             pltpu.VMEM((3, 16, HALF), bf16),
             pltpu.SemaphoreType.DMA((5, 4)),
-            pltpu.SemaphoreType.DMA((2, 3)),
             pltpu.SemaphoreType.DMA((2,)),
         ]
         + GATHER_SEMS
         + REDUCE_SEMS
         + GATHER_SEMS,
-        compiler_params=pltpu.CompilerParams(collective_id=0, has_side_effects=True, vmem_limit_bytes=63 << 20),
+        compiler_params=pltpu.CompilerParams(collective_id=0, has_side_effects=True, vmem_limit_bytes=57 << 20),
         name="distill",
-    )(rows, tgain, sgain, eg, eu, ed, sg, su, sd)
+    )(tokens, ids, weights, tgain, sgain, eg, eu, ed, sg, su, sd)
 
 
 def body(
     tokens, teacher_gain, student_gain, expert_ids, route_weights,
     expert_gate, expert_up, expert_down, student_gate, student_up, student_down,
 ):
-    wide = tokens.astype(jnp.float32)
-    scale = lax.rsqrt(jnp.mean(wide * wide, axis=-1, keepdims=True) + EPSILON)
-    hits = expert_ids[:, :, None] == jnp.arange(64, dtype=jnp.int32)[None, None, :]
-    table = jnp.sum(jnp.where(hits, route_weights[:, :, None], 0.0), axis=1)
-    meta = jnp.concatenate([table, jnp.broadcast_to(scale, (8, 64))], axis=1)
-    meta_high = lax.reduce_precision(meta, 8, 7)
-    rows = jnp.stack(
-        [
-            jnp.concatenate([wide[:, :HALF], meta_high], axis=1),
-            jnp.concatenate([wide[:, HALF:], meta - meta_high], axis=1),
-        ]
+    gate, up, down = step(
+        tokens, expert_ids, route_weights, teacher_gain.reshape(32, 128), student_gain.reshape(32, 128),
+        expert_gate[0], expert_up[0], expert_down[0], student_gate.T, student_up.T, student_down,
     )
-    return step(
-        rows, teacher_gain.reshape(32, 128), student_gain.reshape(32, 128),
-        expert_gate[0], expert_up[0], expert_down[0], student_gate, student_up, student_down,
-    )
+    return gate.T, up.T, down
 
 
 def solution(mesh):

time: 150 us -> 115 us (0.77)
  Pallas kernels: 129 us -> 111 us
  local copies, waits for them, and re-layouts: 17.2 us -> 3.69 us
  other arithmetic: 2.56 us -> 0 us
    pallas_call x1, Pallas kernels: 129 us -> 111 us  [step(): pl.pallas_call(step_kernel, out_shape=(pltpu.VMEM((FU, D), bf16),) * 3, i...]
    pallas_call x2 -> x0, local copies, waits for them, and re-layouts: 6.93 us -> none  [step(): pl.pallas_call(step_kernel, out_shape=(jax.ShapeDtypeStruct((D, FU), bf16...]
    unnamed x7 -> x3, local copies, waits for them, and re-layouts: 9.4 us -> 3.69 us
    reduce_sum x2 -> x0, other arithmetic: 1.79 us -> none  [the longest x1 0.99 us: body(): scale = lax.rsqrt(jnp.mean(wide * wide, axis=-1, keepdims=True) + EPSILON)]
where the time goes in v3:
time: 115 us
  Pallas kernels  111 us (97%)
  local copies, waits for them, and re-layouts  3.69 us (3%)
    pallas_call x1, Pallas kernels, step(): pl.pallas_call(step_kernel, out_shape=(pltpu.VMEM((FU, D), bf16),) * 3, i...  111 us
    unnamed x3, local copies, waits for them, and re-layouts  3.69 us

profile of v3, /device:TPU:1, one launch (start us, length us, event | category | flops | bytes accessed | tf_op | source)
XLA Modules:
  0.0 114.9 jit_solution(10195084129298394120)
XLA Ops:
  0.6 110.6 %distill.1 = (bf16[224,4096]{1,0:T(8,128)(2,1)S(1)}, bf16[224,4096]{1,0:T(8,128)(2,1)S(1)}, bf16[224,4096]{1,0:T(8,128)(2,1)S(1)}) custom-call(bf16[8,4096]{1,0:T(8,128)(2,1)} %tokens_ref.1, s32[8,8]{1,0:T(8,128)} %ids_ref.1, f32[8,8]{1,0:T(8,128)} %weights_ref.1, f32[32,128]{1,0:T(8,128)} %bitcast.16, f32[32,128]{1,0:T(8,128)} %bitcast.17, ...), custom_call_target="tpu_custom_call" | custom-call | tf_op jit(solution)/shard_map/distill/pallas_call | solution.py:591
  111.2 1.2 %copy.17 = bf16[4096,224]{0,1:T(8,128)(2,1)} copy(bf16[4096,224]{0,1:T(8,128)(2,1)S(1)} %bitcast.10) | data formatting | bytes 3670016
  112.5 1.2 %copy.18 = bf16[4096,224]{0,1:T(8,128)(2,1)} copy(bf16[4096,224]{0,1:T(8,128)(2,1)S(1)} %bitcast.9) | data formatting | bytes 3670016
  113.7 1.2 %copy.19 = bf16[224,4096]{1,0:T(8,128)(2,1)} copy(bf16[224,4096]{1,0:T(8,128)(2,1)S(1)} %get-tuple-element.11) | data formatting | bytes 3670016

commit v4 on v3

--- a/solution.py
+++ b/solution.py
@@ -531,12 +531,23 @@
             backward(p, g)
 
     outs.send_blocks()
+    ins.finish()
     outs.send_rows()
+    red.finish()
     outs.take_row(1)
     outs.take_row(2)
-    outs.pass_on(0)
     outs.take_row(3)
     outs.cross(0)
+
+    @pl.loop(0, 4)
+    def _(x):
+        row_scale, _ = facts(x)
+        gate, up = acc_gate[x].reshape(256, FU), acc_up[x].reshape(256, FU)
+        sigma = jax.nn.sigmoid(gate)
+        acc_gate[x] = (row_scale * up * sigma * (1.0 + gate * (1.0 - sigma))).reshape(4, 4, 16, FU)
+        acc_up[x] = (row_scale * gate * sigma).reshape(4, 4, 16, FU)
+
+    outs.pass_on(0)
     outs.pass_on(1)
     back(0)
     outs.pass_on(2)
@@ -550,19 +561,15 @@
     outs.take_far(3)
     outs.cross(3)
     back(2)
+    outs.finish()
     back(3)
 
     @pl.loop(0, 4)
     def _(x):
-        row_scale, _ = facts(x)
-        gate, up = acc_gate[x].reshape(256, FU), acc_up[x].reshape(256, FU)
-        sigma = jax.nn.sigmoid(gate)
-        grad = grad_hidden[x].reshape(256, FU) * row_scale
-        gate_part = grad * up * sigma * (1.0 + gate * (1.0 - sigma))
-        up_part = grad * gate * sigma
+        grad = grad_hidden[x].reshape(256, FU)
         cols = pl.ds(pl.multiple_of(x * 256, 256), 256)
-        pre_t[pl.ds(0, FU), cols] = gate_part.T.astype(jnp.bfloat16)
-        pre_t[pl.ds(FU, FU), cols] = up_part.T.astype(jnp.bfloat16)
+        pre_t[pl.ds(0, FU), cols] = (grad * acc_gate[x].reshape(256, FU)).T.astype(jnp.bfloat16)
+        pre_t[pl.ds(FU, FU), cols] = (grad * acc_up[x].reshape(256, FU)).T.astype(jnp.bfloat16)
 
     for h in range(2):
         for t in range(HALF // 512):
@@ -579,10 +586,6 @@
                 hidden_t[...], g_buf[h, :, :, :, :, cols].reshape(TOKENS, 512), preferred_element_type=jnp.float32
             )
             down_out[:, spot] = value.astype(jnp.bfloat16)
-
-    ins.finish()
-    red.finish()
-    outs.finish()
 
 
 def step(tokens, ids, weights, tgain, sgain, eg, eu, ed, sg, su, sd):

time: 115 us -> 114 us (level)
  Pallas kernels: 111 us -> 109 us
    pallas_call x1, Pallas kernels: 111 us -> 109 us  [step(): pl.pallas_call(step_kernel, out_shape=(pltpu.VMEM((FU, D), bf16),) * 3, i...]
where the time goes in v4:
time: 114 us
  Pallas kernels  109 us (96%)
  local copies, waits for them, and re-layouts  3.69 us (3%)
    pallas_call x1, Pallas kernels, step(): pl.pallas_call(step_kernel, out_shape=(pltpu.VMEM((FU, D), bf16),) * 3, i...  109 us
    unnamed x3, local copies, waits for them, and re-layouts  3.69 us

profile of v4, /device:TPU:1, one launch (start us, length us, event | category | flops | bytes accessed | tf_op | source)
XLA Modules:
  0.0 113.7 jit_solution(9305488019713392957)
XLA Ops:
  0.6 109.4 %distill.1 = (bf16[224,4096]{1,0:T(8,128)(2,1)S(1)}, bf16[224,4096]{1,0:T(8,128)(2,1)S(1)}, bf16[224,4096]{1,0:T(8,128)(2,1)S(1)}) custom-call(bf16[8,4096]{1,0:T(8,128)(2,1)} %tokens_ref.1, s32[8,8]{1,0:T(8,128)} %ids_ref.1, f32[8,8]{1,0:T(8,128)} %weights_ref.1, f32[32,128]{1,0:T(8,128)} %bitcast.16, f32[32,128]{1,0:T(8,128)} %bitcast.17, ...), custom_call_target="tpu_custom_call" | custom-call | tf_op jit(solution)/shard_map/distill/pallas_call | solution.py:594
  110.0 1.2 %copy.17 = bf16[4096,224]{0,1:T(8,128)(2,1)} copy(bf16[4096,224]{0,1:T(8,128)(2,1)S(1)} %bitcast.10) | data formatting | bytes 3670016
  111.2 1.2 %copy.18 = bf16[4096,224]{0,1:T(8,128)(2,1)} copy(bf16[4096,224]{0,1:T(8,128)(2,1)S(1)} %bitcast.9) | data formatting | bytes 3670016
  112.5 1.2 %copy.19 = bf16[224,4096]{1,0:T(8,128)(2,1)} copy(bf16[224,4096]{1,0:T(8,128)(2,1)S(1)} %get-tuple-element.11) | data formatting | bytes 3670016

commit v5 on v4

--- a/solution.py
+++ b/solution.py
@@ -316,7 +316,7 @@
 def step_kernel(
     tokens_ref, ids_ref, weights_ref, tgain_ref, sgain_ref, eg, eu, ed, sg, su, sd, gate_out, up_out, down_out,
     x_buf, g_buf, total, pair_buf, w_teacher, down, acc_teacher, acc_gate, acc_up, grad_hidden,
-    hid, hidden_t, pre_t, rows, other, box0, box1, box2, row_boxes, block_boxes, load_sem, first_sem, *sems
+    hid, hidden, down_sum, pre_t, rows, other, box0, box1, box2, row_boxes, block_boxes, load_sem, first_sem, *sems
 ):
     place = Place()
     core = place.core
@@ -468,7 +468,7 @@
         acc_gate[x] = gate.reshape(4, 4, 16, FU)
         acc_up[x] = up.reshape(4, 4, 16, FU)
         value = gate * jax.nn.sigmoid(gate) * up
-        hidden_t[:, pl.ds(pl.multiple_of(x * 256, 256), 256)] = value.T.astype(jnp.bfloat16)
+        hidden[x] = value.astype(jnp.bfloat16).reshape(4, 4, 16, FU)
         half = jnp.where(place.grp == 0, value[:, :OWN], value[:, OWN:])
         half = jnp.concatenate([half, jnp.zeros((256, 128 - OWN), jnp.float32)], axis=1)
         hid[x, :, :, :, pl.ds(FE, 128)] = half.astype(jnp.bfloat16).reshape(4, 4, 16, 128)
@@ -523,6 +523,17 @@
         ).reshape(4, 4, 16, FU)
         grad_hidden[index] = grad_hidden[index] + value
 
+    def down_part(p, gs, h):
+        low, _, high = OUT_PARTS[p]
+        width = high - low
+        groups = [place.group(p, ROWS_OUT[g]) for g in gs]
+        lhs = jnp.concatenate([hidden[i + (slice(None), slice(None))].reshape(256, FU) for i in groups], axis=0)
+        rhs = jnp.concatenate(
+            [g_buf[(h,) + i + (slice(None), pl.ds(low, width))].reshape(256, width) for i in groups], axis=0
+        )
+        value = lax.dot_general(lhs, rhs, (((0,), (0,)), ((), ())), preferred_element_type=jnp.float32)
+        return pl.ds(h * HALF + low, width), value
+
     outs = Gather(place, g_buf, OUT_PARTS, sems[9:14])
 
     def back(g):
@@ -554,13 +565,15 @@
     outs.pass_on(3)
     outs.cross(1)
     outs.cross(2)
-    outs.take_far(0)
-    outs.take_far(1)
     back(1)
-    outs.take_far(2)
-    outs.take_far(3)
+    back(2)
+    for p in range(3):
+        for h in range(2):
+            cols, value = down_part(p, (0, 1, 2), h)
+            down_sum[:, cols] = value
+    for r in range(4):
+        outs.take_far(r)
     outs.cross(3)
-    back(2)
     outs.finish()
     back(3)
 
@@ -571,6 +584,10 @@
         pre_t[pl.ds(0, FU), cols] = (grad * acc_gate[x].reshape(256, FU)).T.astype(jnp.bfloat16)
         pre_t[pl.ds(FU, FU), cols] = (grad * acc_up[x].reshape(256, FU)).T.astype(jnp.bfloat16)
 
+    for p in range(3):
+        for h in range(2):
+            cols, value = down_part(p, (3,), h)
+            down_out[:, cols] = (down_sum[:, cols] + value).astype(jnp.bfloat16)
     for h in range(2):
         for t in range(HALF // 512):
             cols = pl.ds(t * 512, 512)
@@ -582,10 +599,6 @@
             gain = jnp.concatenate([sgain_ref[first_gain + i:first_gain + i + 1, :] for i in range(4)], axis=1)
             gate_out[:, spot] = (value[:FU] * gain).astype(jnp.bfloat16)
             up_out[:, spot] = (value[FU:] * gain).astype(jnp.bfloat16)
-            value = jnp.dot(
-                hidden_t[...], g_buf[h, :, :, :, :, cols].reshape(TOKENS, 512), preferred_element_type=jnp.float32
-            )
-            down_out[:, spot] = value.astype(jnp.bfloat16)
 
 
 def step(tokens, ids, weights, tgain, sgain, eg, eu, ed, sg, su, sd):
@@ -608,7 +621,8 @@
             pltpu.VMEM((4, 4, 4, 16, FU), f32),
             pltpu.VMEM((4, 4, 4, 16, FU), f32),
             pltpu.VMEM((4, 4, 4, 16, 512), bf16),
-            pltpu.VMEM((FU, TOKENS), bf16),
+            pltpu.VMEM((4, 4, 4, 16, FU), bf16),
+            pltpu.VMEM((FU, D), f32),
             pltpu.VMEM((2 * FU, TOKENS), bf16),
             pltpu.VMEM((2, 8, WIDE), f32),
             pltpu.VMEM((8, WIDE), f32),

time: 114 us -> 116 us (1.018)
  Pallas kernels: 109 us -> 111 us
    pallas_call x1, Pallas kernels: 109 us -> 111 us  [step(): pl.pallas_call(step_kernel, out_shape=(pltpu.VMEM((FU, D), bf16),) * 3, i...]
where the time goes in v5:
time: 116 us
  Pallas kernels  111 us (96%)
  local copies, waits for them, and re-layouts  3.69 us (3%)
    pallas_call x1, Pallas kernels, step(): pl.pallas_call(step_kernel, out_shape=(pltpu.VMEM((FU, D), bf16),) * 3, i...  111 us
    unnamed x3, local copies, waits for them, and re-layouts  3.69 us

profile of v5, /device:TPU:1, one launch (start us, length us, event | category | flops | bytes accessed | tf_op | source)
XLA Modules:
  0.0 115.5 jit_solution(17815450643588361579)
XLA Ops:
  0.6 111.2 %distill.1 = (bf16[224,4096]{1,0:T(8,128)(2,1)S(1)}, bf16[224,4096]{1,0:T(8,128)(2,1)S(1)}, bf16[224,4096]{1,0:T(8,128)(2,1)S(1)}) custom-call(bf16[8,4096]{1,0:T(8,128)(2,1)} %tokens_ref.1, s32[8,8]{1,0:T(8,128)} %ids_ref.1, f32[8,8]{1,0:T(8,128)} %weights_ref.1, f32[32,128]{1,0:T(8,128)} %bitcast.16, f32[32,128]{1,0:T(8,128)} %bitcast.17, ...), custom_call_target="tpu_custom_call" | custom-call | tf_op jit(solution)/shard_map/distill/pallas_call | solution.py:607
  111.8 1.2 %copy.17 = bf16[4096,224]{0,1:T(8,128)(2,1)} copy(bf16[4096,224]{0,1:T(8,128)(2,1)S(1)} %bitcast.10) | data formatting | bytes 3670016
  113.1 1.2 %copy.18 = bf16[4096,224]{0,1:T(8,128)(2,1)} copy(bf16[4096,224]{0,1:T(8,128)(2,1)S(1)} %bitcast.9) | data formatting | bytes 3670016
  114.3 1.2 %copy.19 = bf16[224,4096]{1,0:T(8,128)(2,1)} copy(bf16[224,4096]{1,0:T(8,128)(2,1)S(1)} %get-tuple-element.11) | data formatting | bytes 3670016
